TPU v7x, 32 devices: a whole 2x2x4 slice. The times are simulated.
32 devices in a mesh: groups: 2 (over x), track: 4 (over y, core), frame: 4 (over z).
Axes of the slice: x: 2, y: 2, z: 4, core: 2. Of those that a mesh axis runs over, the one named last changes fastest.
Arguments:
- frames: bfloat16 [16, 4096, 256], P(('groups', 'frame')), parts along dimension 0, may hold values from -9 to 9
- query_frame: int32 [1024], P(('groups', 'track')), parts along dimension 0, may hold values from 0 to 7
- query_pixel: int32 [1024], P(('groups', 'track')), parts along dimension 0, may hold values from 0 to 4095
- cotangent: float32 [2, 16, 512], P(None, ('groups', 'frame'), 'track'), parts along dimension 1, may hold values from -48 to 48
Outputs:
- frame_grad: float32 [4096, 16, 256], P('track', ('groups', 'frame')), parts along dimension 1
- query_grad: float32 [1024, 256], P(('groups', 'track', 'frame')), parts along dimension 0
There are 2 independent parts, one for each index of `groups`. A program takes and returns all parts, laid end to end along the dimension named above; each array names one. Nothing has to cross between parts.
All inputs are finite; a program needn't handle non-finite values.
Results may differ from a plain program's by a relative error of at most 0.0029.
Values may be sent and summed in bfloat16 or wider, within the bound.
A program may use at most 64 MiB of HBM per device.

v0:
```python
import jax
import jax.numpy as jnp
from jax import lax
from jax.sharding import PartitionSpec as P

C = 256
FEAT_H = 64
FEAT_W = 64


def on_device(frames, query_frame, query_pixel, cotangent):
    held_frames = frames.shape[0]
    pixels = frames.shape[1]
    channels = frames.shape[2]
    offset = lax.axis_index("frame") * held_frames
    local_index = query_frame - offset
    inside = (local_index >= 0) & (local_index < held_frames)
    row_index = jnp.clip(local_index, 0, held_frames - 1) * pixels + query_pixel
    picked = frames.reshape(held_frames * pixels, channels)[row_index]
    picked = jnp.where(inside[:, None], picked.astype(jnp.float32), 0.0)
    query_feat = lax.psum(picked.astype(jnp.bfloat16), "frame")
    score_scale = C ** (-0.5)
    pixel_ids = jnp.arange(pixels)
    coord_x = (pixel_ids % FEAT_W * (2.0 / (FEAT_W - 1)) - 1.0).astype(jnp.float32)
    coord_y = (pixel_ids // FEAT_W * (2.0 / (FEAT_H - 1)) - 1.0).astype(jnp.float32)
    scores = (
        jnp.einsum("qc,tpc->tqp", query_feat, frames, preferred_element_type=jnp.float32)
        * score_scale
    )
    peak_score = jnp.max(scores, axis=2, keepdims=True)
    exp_scores = jnp.exp(scores - peak_score)
    weights = exp_scores / jnp.sum(exp_scores, axis=2, keepdims=True)
    expect_x = jnp.sum(weights * coord_x, axis=2)
    expect_y = jnp.sum(weights * coord_y, axis=2)
    grad_x = cotangent[0]
    grad_y = cotangent[1]
    inner_sum = grad_x * expect_x + grad_y * expect_y
    cost_grad = (
        weights
        * (grad_x[:, :, None] * coord_x + grad_y[:, :, None] * coord_y - inner_sum[:, :, None])
        * score_scale
    ).astype(jnp.bfloat16)
    query_term = jnp.einsum("tqp,tpc->qc", cost_grad, frames, preferred_element_type=jnp.float32)
    query_grad = lax.psum_scatter(query_term, "frame", scatter_dimension=0, tiled=True)
    everyone = lax.all_gather(query_feat, "track", axis=0, tiled=True)
    frame_grad = jnp.einsum(
        "tqp,qc->ptc",
        lax.all_to_all(cost_grad, "track", split_axis=2, concat_axis=1, tiled=True),
        everyone,
        preferred_element_type=jnp.float32,
    )
    return (frame_grad, query_grad)


def solution(mesh):
    return jax.shard_map(
        on_device,
        mesh=mesh,
        in_specs=(
            P(("groups", "frame"), None, None),
            P(("groups", "track")),
            P(("groups", "track")),
            P(None, ("groups", "frame"), "track"),
        ),
        out_specs=(P("track", ("groups", "frame"), None), P(("groups", "track", "frame"), None)),
        check_vma=False,
    )
```

profile of v0, /device:TPU:0, one launch (start us, length us, event | category | flops | bytes accessed | tf_op | source)
XLA Modules:
  0.0 114.0 jit_solution(15682147279452416401)
XLA Ops:
  7.2 0.0 all-reduce.2.cloned.1.call-start
  7.2 0.7 compare_and_fusion
  7.9 0.7 compare_select_fusion
  8.6 3.5 %gather_fusion = bf16[128,256]{1,0:T(8,128)(2,1)S(1)} fusion(bf16[8192,256]{1,0:T(8,128)(2,1)} %bitcast.38, s32[1024]{0:T(1024)S(1)} %pad_clamp_fusion), kind=kCustom, calls=%fused_computation | custom fusion | bytes 131584 | tf_op jit(solution)/shard_map/gather | solution.py:19
  12.1 0.7 select_convert_fusion
  12.8 0.0 all-reduce.2.cloned.1.call-update
  12.8 0.7 slice_bitcast_fusion.1
  13.5 36.1 %all-reduce.2.cloned.1.call-done = bf16[128,256]{1,0:T(8,128)(2,1)} async-done(((bf16[128,256]{1,0:T(8,128)(2,1)}), bf16[128,256]{1,0:T(8,128)(2,1)}) %all-reduce.2.cloned.1.call-update) | async-done | bytes 65552 | tf_op jit(solution)/shard_map/psum | solution.py:21
  49.6 0.0 copy-start.1
  49.6 7.0 %multiply_reduce_fusion.1 = (f32[2,128]{1,0:T(2,128)S(1)}, f32[2,128]{1,0:T(2,128)S(1)}, f32[2,128,4096]{2,1,0:T(8,128)}) fusion(f32[4096]{0:T(1024)S(1)} %get-tuple-element.11, f32[4096]{0:T(1024)S(1)} %get-tuple-element.12, bf16[2,4096,256]{2,1,0:T(8,128)(2,1)} %param.4, bf16[128,256]{1,0:T(8,128)(2,1)} %all-reduce.2.cloned.1.call-done), kind=kOutput, calls=%fused_computation.10 | convolution fusion | flops 544219136 | bytes 8488960 | tf_op jit(solution)/shard_map/div | solution.py:32
  56.7 0.0 copy-done.1
  56.7 3.5 %multiply_convert_fusion = bf16[2,128,4096]{2,1,0:T(8,128)(2,1)S(1)} fusion(f32[2,128,4096]{2,1,0:T(8,128)} %get-tuple-element.10, f32[2,128]{1,0:T(2,128)S(1)} %multiply_add_fusion, f32[4096]{0:T(1024)S(1)} %get-tuple-element.12, f32[2,128]{1,0:T(2,128)S(1)} %get-tuple-element.9, f32[4096]{0:T(1024)S(1)} %get-tuple-element.11, f32[2,128]{1,0:T(2,128)S(1)} %get-tuple-element.8), kind=kLoop, calls=%fused_computation.8 | loop fusion | flops 7340032 | bytes 6327296 | tf_op jit(solution)/shard_map/convert_element_type | solution.py:42
  60.1 3.8 %copy.9 = bf16[2,128,4096]{1,0,2:T(2,128)(2,1)} copy(bf16[2,128,4096]{2,1,0:T(8,128)(2,1)S(1)} %multiply_convert_fusion) | data formatting | bytes 4194304 | tf_op jit(solution)/shard_map/convert_element_type | solution.py:42
  63.9 4.4 %all-to-all-start = ((bf16[2,128,4096]{1,0,2:T(2,128)(2,1)}), bf16[2,128,4096]{1,0,2:T(2,128)(2,1)}, u32[]{:S(2)}, u32[]{:S(2)}) async-start(bf16[2,128,4096]{1,0,2:T(2,128)(2,1)} %copy.9), calls=%async_computation | async-start | bytes 4194304 | tf_op jit(solution)/shard_map/all_to_all | solution.py:48
  68.4 0.0 copy-start
  68.4 0.0 reduce-scatter.2.cloned.1.call-start
  68.4 3.6 %convolution_bitcast_fusion.1 = f32[128,256]{1,0:T(8,128)} fusion(bf16[2,128,4096]{2,1,0:T(8,128)(2,1)S(1)} %multiply_convert_fusion, bf16[2,4096,256]{2,1,0:T(8,128)(2,1)} %param.4), kind=kOutput, calls=%fused_computation.12 | convolution fusion | flops 536870912 | bytes 6422528 | tf_op jit(solution)/shard_map/tqp,tpc->qc/dot_general | solution.py:43
  72.0 0.0 reduce-scatter.2.cloned.1.call-update
  72.0 0.0 copy-done
  72.0 24.2 %all_gather.3 = bf16[512,256]{1,0:T(8,128)(2,1)S(1)} all-gather(bf16[128,256]{1,0:T(8,128)(2,1)S(1)} %copy-done), channel_id=1, replica_groups=mesh['groups'=2,'track'=4,'frame'=4] {'track'}, dimensions={0}, use_global_device_ids=true | all-gather | bytes 327680 | tf_op jit(solution)/shard_map/all_gather | solution.py:45
  96.3 0.0 all-to-all-done
  96.3 4.7 %copy.10 = bf16[2,128,4,1024]{3,1,2,0:T(8,128)(2,1)S(1)} copy(bf16[2,128,4,1024]{1,0,3,2:T(2,128)(2,1)} %bitcast.6) | data formatting | bytes 4194304 | tf_op jit(solution)/shard_map/all_to_all | solution.py:48
  101.0 2.1 %convolution_bitcast_fusion = f32[1024,2,256]{0,2,1:T(8,128)} fusion(bf16[2,512,1024]{2,1,0:T(8,128)(2,1)S(1)} %bitcast.37, bf16[512,256]{1,0:T(8,128)(2,1)S(1)} %all_gather.3), kind=kOutput, calls=%fused_computation.11 | convolution fusion | flops 536870912 | bytes 4456448 | tf_op jit(solution)/shard_map/tqp,qc->ptc/dot_general | solution.py:46
  103.1 4.1 %copy.12 = f32[1024,2,256]{2,1,0:T(2,128)} copy(f32[1024,2,256]{0,2,1:T(8,128)} %convolution_bitcast_fusion) | data formatting | bytes 4194304
  (4 shorter events, 0.0 us)
Async XLA Ops:
  7.2 42.5 %all-reduce.2.cloned.1.call-start = ((), (), s32[]{:S(2)}) async-start(), calls=%async_computation.2 | async-start | bytes 131072 | tf_op jit(solution)/shard_map/psum | solution.py:21
  49.6 7.0 %copy-start.1 = (f32[2,2,128]{2,1,0:T(2,128)S(1)}, f32[2,2,128]{2,1,0:T(2,128)}, u32[]{:S(2)}) copy-start(f32[2,2,128]{2,1,0:T(2,128)} %param.7) | copy-start | bytes 6148
  63.9 32.4 %all-to-all-start = ((bf16[2,128,4096]{1,0,2:T(2,128)(2,1)}), bf16[2,128,4096]{1,0,2:T(2,128)(2,1)}, u32[]{:S(2)}, u32[]{:S(2)}) async-start(bf16[2,128,4096]{1,0,2:T(2,128)(2,1)} %copy.9), calls=%async_computation | async-start | bytes 4194304 | tf_op jit(solution)/shard_map/all_to_all | solution.py:48
  68.4 3.6 %copy-start = (bf16[128,256]{1,0:T(8,128)(2,1)S(1)}, bf16[128,256]{1,0:T(8,128)(2,1)}, u32[]{:S(2)}) copy-start(bf16[128,256]{1,0:T(8,128)(2,1)} %all-reduce.2.cloned.1.call-done) | copy-start | bytes 196612
  68.4 38.8 %reduce-scatter.2.cloned.1.call-start = ((), (), s32[]{:S(2)}) async-start(), calls=%async_computation.3 | async-start | bytes 163840 | tf_op jit(solution)/shard_map/reduce_scatter | solution.py:44
Sparse Core Ops, SparseCore 0:
  12.9 36.6 all-reduce.1
  72.1 19.3 reduce-scatter.1
where the time goes:
time: 115 us; the launch traced here: 114 us
  waiting for transfers between devices  36.2 us (31%)
  blocking collectives  24.2 us (21%)
  local copies, waits for them, and re-layouts  16.8 us (15%)
  between operations  14.1 us (12%)
  matrix products  12.7 us (11%)
  other arithmetic  5.55 us (5%)
  starting transfers between devices  4.52 us (4%)
    psum x1, waiting for transfers between devices, on_device(): query_feat = lax.psum(picked.astype(jnp.bfloat16), 'frame')  36.1 us
    all_gather x1, blocking collectives, on_device(): everyone = lax.all_gather(query_feat, 'track', axis=0, tiled=True)  24.2 us
    div x1, matrix products, on_device(): weights = exp_scores / jnp.sum(exp_scores, axis=2, keepdims=True)  7.02 us
    all_to_all x1, local copies, waits for them, and re-layouts, on_device(): lax.all_to_all(cost_grad, 'track', split_axis=2, concat_axis=1, tiled=True)  4.73 us
    all_to_all x1, starting transfers between devices, on_device(): lax.all_to_all(cost_grad, 'track', split_axis=2, concat_axis=1, tiled=True)  4.44 us
    unnamed x5, local copies, waits for them, and re-layouts  4.12 us
    convert_element_type x1, local copies, waits for them, and re-layouts, on_device(): cost_grad = (weights * (grad_x[:, :, None] * coord_x + grad_y[:, :, None]...  3.77 us
    dot_general x1, matrix products, on_device(): jnp.einsum('tqp,tpc->qc', cost_grad, frames, preferred_element_type=jnp.f...  3.56 us
  transfers between devices with their start and end apart: 3, of which 1 were waited for; matrix products, arithmetic and copies ran while one was open for 13% of the time, Pallas kernels for 0%

commit v1 on v0

v1 whole, which is shorter than its diff:
```python
import functools
import math

import jax
import jax.numpy as jnp
from jax import lax
from jax.experimental import pallas as pl
from jax.experimental.pallas import tpu as pltpu
from jax.sharding import PartitionSpec as P

C = 256
FEAT_H = 64
FEAT_W = 64
LANES = 128
MESH = pl.DeviceIdType.MESH
SCORE_SCALE = C ** (-0.5)
LOG2_SCALE = SCORE_SCALE * math.log2(math.e)
STEP_X = 2.0 / (FEAT_W - 1)
STEP_Y = 2.0 / (FEAT_H - 1)


def dot(a, b, dims):
    return lax.dot_general(a, b, (dims, ((), ())), preferred_element_type=jnp.float32)


def kernel(
    n_track,
    n_frame,
    frames_hbm,
    query_frame_ref,
    query_pixel_ref,
    cot_ref,
    out_ref,
    query_out_ref,
    fr,
    scores,
    picked,
    picked_in,
    feats,
    stats,
    term,
    term_in,
    load_sem,
    pick_send,
    pick_recv,
    ring_send,
    ring_recv,
    feat_send,
    feat_recv,
    stat_send,
    stat_recv,
    term_send,
    term_recv,
):
    held, pixels, channels = fr.shape
    q = cot_ref.shape[2]
    rows = q // n_frame
    block = pixels // n_track
    me_t = lax.axis_index("track")
    me_f = lax.axis_index("frame")

    def peers(name, me, n):
        return [(d, {name: lax.rem(me + d, n)}) for d in range(1, n)]

    track_peers = peers("track", me_t, n_track)
    frame_peers = peers("frame", me_f, n_frame)

    barrier = pltpu.get_barrier_semaphore()
    for _, device in track_peers + frame_peers:
        pl.semaphore_signal(barrier, inc=1, device_id=device, device_id_type=MESH)

    parts = load_sem.shape[1]
    piece = pixels // parts
    loads = []
    for t in range(held):
        for i in range(parts):
            where = pl.ds(i * piece, piece)
            load = pltpu.make_async_copy(frames_hbm.at[t, where], fr.at[t, where], load_sem.at[t, i])
            load.start()
            loads.append((t, i, load))

    eye = lax.broadcasted_iota(jnp.int32, (q, q), 0) == lax.broadcasted_iota(jnp.int32, (q, q), 1)

    def to_column(row):
        return jnp.sum(jnp.where(eye, row, jnp.zeros_like(row)), axis=1, keepdims=True)

    def to_row(column):
        return jnp.sum(jnp.where(eye, column, jnp.zeros_like(column)), axis=0, keepdims=True)

    index = (query_frame_ref[...] - me_f * held) * pixels + query_pixel_ref[...]
    index = to_column(index.astype(jnp.float32)).astype(jnp.int32)
    lane = lax.broadcasted_iota(jnp.int32, (q, piece), 1)
    total = jnp.zeros((q, channels), jnp.float32)
    for t, i, load in loads:
        load.wait()
        hot = jnp.where(lane == index - (t * pixels + i * piece), 1.0, 0.0).astype(jnp.bfloat16)
        total += dot(hot, fr[t, i * piece : (i + 1) * piece, :], ((1,), (0,)))
    picked[...] = total.astype(jnp.bfloat16).reshape(n_frame, rows, channels)

    pl.semaphore_wait(barrier, n_track + n_frame - 2)

    copies = []
    for d, device in frame_peers:
        copies.append(
            pltpu.make_async_remote_copy(
                src_ref=picked.at[lax.rem(me_f + d, n_frame)],
                dst_ref=picked_in.at[d],
                send_sem=pick_send.at[d],
                recv_sem=pick_recv.at[d],
                device_id=device,
                device_id_type=MESH,
            )
        )
        copies[-1].start()
    mine = picked[me_f].astype(jnp.float32)
    for d, copy in enumerate(copies, 1):
        copy.wait_recv()
        mine += picked_in[d].astype(jnp.float32)
    feats[me_t, me_f] = mine.astype(jnp.bfloat16)
    sends = copies
    copies = []
    for d, device in frame_peers:
        copies.append(
            pltpu.make_async_remote_copy(
                src_ref=feats.at[me_t, me_f],
                dst_ref=feats.at[me_t, me_f],
                send_sem=ring_send.at[d],
                recv_sem=ring_recv.at[d],
                device_id=device,
                device_id_type=MESH,
            )
        )
        copies[-1].start()
    for copy in copies:
        copy.wait_recv()
    sends += copies
    feat_copies = []
    for d, device in track_peers:
        feat_copies.append(
            pltpu.make_async_remote_copy(
                src_ref=feats.at[me_t],
                dst_ref=feats.at[me_t],
                send_sem=feat_send.at[d],
                recv_sem=feat_recv.at[d],
                device_id=device,
                device_id_type=MESH,
            )
        )
        feat_copies[-1].start()
    sends += feat_copies

    own = feats[me_t].reshape(q, channels)
    wide = scores.shape[3]
    cols = wide // LANES
    chunks = pixels // wide
    lane = lax.broadcasted_iota(jnp.int32, (q, LANES), 1)
    lane_x = (lane % FEAT_W).astype(jnp.float32)
    lane_y = (lane // FEAT_W).astype(jnp.float32)
    row_step = LANES // FEAT_W

    def split(x):
        return [x[:, c * LANES : (c + 1) * LANES] for c in range(cols)]

    def chunk_of(t, i):
        return fr[t, pl.ds(pl.multiple_of(i * wide, wide), wide), :]

    peaks = []
    for t in range(held):

        def score(i, peak):
            s = dot(own, chunk_of(t, i), ((1,), (1,)))
            scores[t, i] = s
            return functools.reduce(jnp.maximum, split(s), peak)

        peak = lax.fori_loop(0, chunks, score, jnp.full((q, LANES), -jnp.inf, jnp.float32))
        peaks.append(jnp.max(peak, axis=1, keepdims=True) * LOG2_SCALE)

    columns = []
    for t in range(held):

        def expo(i, carry):
            zero, first = carry
            e = jnp.exp2(scores[t, i] * LOG2_SCALE - peaks[t])
            scores[t, i] = e
            e = split(e)
            tail = e[-1]
            moment = tail
            for part in e[-2:0:-1]:
                tail = tail + part
                moment = moment + tail
            tail = tail + e[0]
            return zero + tail, first + (moment + tail * (i * cols).astype(jnp.float32))

        empty = jnp.zeros((q, LANES), jnp.float32)
        zero, first = lax.fori_loop(0, chunks, expo, (empty, empty))
        mass = jnp.sum(zero, axis=1, keepdims=True)
        mean_x = jnp.sum(zero * lane_x, axis=1, keepdims=True) / mass
        mean_y = jnp.sum(zero * lane_y + first * row_step, axis=1, keepdims=True) / mass
        grad_x = to_column(cot_ref[0, t : t + 1, :])
        grad_y = to_column(cot_ref[1, t : t + 1, :])
        scale = SCORE_SCALE / mass
        slope_x = grad_x * STEP_X * scale
        slope_y = grad_y * STEP_Y * scale
        columns.append((slope_x, slope_y, -(slope_x * mean_x + slope_y * mean_y)))

    for t in range(held):
        for i, column in enumerate((peaks[t],) + columns[t]):
            stats[me_t, 4 * t + i : 4 * t + i + 1, :] = to_row(column)
    stat_copies = []
    for d, device in track_peers:
        stat_copies.append(
            pltpu.make_async_remote_copy(
                src_ref=stats.at[me_t],
                dst_ref=stats.at[me_t],
                send_sem=stat_send.at[d],
                recv_sem=stat_recv.at[d],
                device_id=device,
                device_id_type=MESH,
            )
        )
        stat_copies[-1].start()
    sends += stat_copies

    total = jnp.zeros((q, channels), jnp.float32)
    for t in range(held):
        slope_x, slope_y, level = columns[t]
        base = level + slope_x * lane_x + slope_y * lane_y
        step = slope_y * row_step

        def query_part(i, total):
            at = [base + step * (i * cols + c).astype(jnp.float32) for c in range(cols)]
            grad = (scores[t, i] * jnp.concatenate(at, axis=1)).astype(jnp.bfloat16)
            return total + dot(grad, chunk_of(t, i), ((1,), (0,)))

        total = lax.fori_loop(0, chunks, query_part, total)
    term[...] = total.reshape(n_frame, rows, channels)
    term_copies = []
    for d, device in frame_peers:
        term_copies.append(
            pltpu.make_async_remote_copy(
                src_ref=term.at[lax.rem(me_f + d, n_frame)],
                dst_ref=term_in.at[d],
                send_sem=term_send.at[d],
                recv_sem=term_recv.at[d],
                device_id=device,
                device_id_type=MESH,
            )
        )
        term_copies[-1].start()
    sends += term_copies

    for copy in feat_copies + stat_copies:
        copy.wait_recv()
    tracks = n_track * q
    everyone = feats[...].reshape(tracks, channels)
    levels = jnp.concatenate([stats[k] for k in range(n_track)], axis=1)
    size = max(FEAT_W, min(block, 131072 // tracks // FEAT_W * FEAT_W))
    lines = size // FEAT_W
    tiles = channels // LANES
    column_x = lax.broadcasted_iota(jnp.int32, (FEAT_W, 1), 0).astype(jnp.float32)
    slopes = [levels[4 * t + 1 : 4 * t + 2] * column_x for t in range(held)]

    def frame_part(i, carry):
        start = me_t * block + i * size
        first_line = me_t * (block // FEAT_W) + i * lines
        for t in range(held):
            peak, _, slope_y, level = [levels[4 * t + j : 4 * t + j + 1] for j in range(4)]
            s = dot(fr[t, pl.ds(pl.multiple_of(start, FEAT_W), size), :], everyone, ((1,), (1,)))
            e = jnp.exp2(s * LOG2_SCALE - peak)
            at = [slopes[t] + (level + slope_y * (first_line + l).astype(jnp.float32)) for l in range(lines)]
            grad = (e * jnp.concatenate(at, axis=0)).astype(jnp.bfloat16)
            result = dot(grad, everyone, ((1,), (0,)))
            for c in range(tiles):
                place = pl.ds(i * (size * tiles * held) + c * held + t, size, stride=tiles * held)
                out_ref[place, :] = result[:, c * LANES : (c + 1) * LANES]
        return carry

    lax.fori_loop(0, block // size, frame_part, 0)

    mine = term[me_f]
    for d, copy in enumerate(term_copies, 1):
        copy.wait_recv()
        mine += term_in[d]
    query_out_ref[...] = mine
    for copy in sends:
        copy.wait_send()


def on_device(n_track, n_frame, frames, query_frame, query_pixel, cotangent):
    held, pixels, channels = frames.shape
    q = query_frame.shape[0]
    rows = q // n_frame
    block = pixels // n_track
    tiles = channels // LANES
    wide = 4 * LANES
    vmem = pl.BlockSpec(memory_space=pltpu.VMEM)
    dma = pltpu.SemaphoreType.DMA
    frame_grad, query_grad = pl.pallas_call(
        functools.partial(kernel, n_track, n_frame),
        out_shape=(
            jax.ShapeDtypeStruct((block * tiles * held, LANES), jnp.float32),
            jax.ShapeDtypeStruct((rows, channels), jnp.float32),
        ),
        in_specs=[pl.BlockSpec(memory_space=pl.ANY), vmem, vmem, vmem],
        out_specs=(vmem, vmem),
        scratch_shapes=[
            pltpu.VMEM((held, pixels, channels), jnp.bfloat16),
            pltpu.VMEM((held, pixels // wide, q, wide), jnp.float32),
            pltpu.VMEM((n_frame, rows, channels), jnp.bfloat16),
            pltpu.VMEM((n_frame, rows, channels), jnp.bfloat16),
            pltpu.VMEM((n_track, n_frame, rows, channels), jnp.bfloat16),
            pltpu.VMEM((n_track, 4 * held, q), jnp.float32),
            pltpu.VMEM((n_frame, rows, channels), jnp.float32),
            pltpu.VMEM((n_frame, rows, channels), jnp.float32),
            dma((held, 4)),
            dma((n_frame,)),
            dma((n_frame,)),
            dma((n_frame,)),
            dma((n_frame,)),
            dma((n_track,)),
            dma((n_track,)),
            dma((n_track,)),
            dma((n_track,)),
            dma((n_frame,)),
            dma((n_frame,)),
        ],
        compiler_params=pltpu.CompilerParams(
            collective_id=0, has_side_effects=True, vmem_limit_bytes=40 * 2**20
        ),
        name="matching_grad",
    )(frames, query_frame.reshape(1, q), query_pixel.reshape(1, q), cotangent)
    frame_grad = frame_grad.reshape(block, tiles, held, LANES).transpose(0, 2, 1, 3)
    return (frame_grad.reshape(block, held, channels), query_grad)


def solution(mesh):
    return jax.shard_map(
        functools.partial(on_device, mesh.shape["track"], mesh.shape["frame"]),
        mesh=mesh,
        in_specs=(
            P(("groups", "frame"), None, None),
            P(("groups", "track")),
            P(("groups", "track")),
            P(None, ("groups", "frame"), "track"),
        ),
        out_specs=(P("track", ("groups", "frame"), None), P(("groups", "track", "frame"), None)),
        check_vma=False,
    )
```

time: 115 us -> 32.4 us (0.28)
  waiting for transfers between devices: 36.2 us -> 0 us
  Pallas kernels: 0 us -> 25.4 us
  blocking collectives: 24.2 us -> 0 us
  between operations: 14.1 us -> 0.65 us
  matrix products: 12.7 us -> 0 us
  local copies, waits for them, and re-layouts: 16.8 us -> 6.11 us
  other arithmetic: 5.55 us -> 0 us
  starting transfers between devices: 4.52 us -> 0 us
    psum x1 -> x0, waiting for transfers between devices: 36.1 us -> none  [on_device(): query_feat = lax.psum(picked.astype(jnp.bfloat16), 'frame')]
    pallas_call x0 -> x1, Pallas kernels: none -> 25.4 us  [on_device(): pl.pallas_call(functools.partial(kernel, n_track, n_frame), out_shape=(ja...]
    all_gather x1 -> x0, blocking collectives: 24.2 us -> none  [on_device(): everyone = lax.all_gather(query_feat, 'track', axis=0, tiled=True)]
    div x1 -> x0, matrix products: 7.02 us -> none  [on_device(): weights = exp_scores / jnp.sum(exp_scores, axis=2, keepdims=True)]
    dot_general x2 -> x0, matrix products: 5.64 us -> none  [the longest x1 3.56 us: on_device(): jnp.einsum('tqp,tpc->qc', cost_grad, frames, preferred_element_type=jnp.f...]
    all_to_all x1 -> x0, local copies, waits for them, and re-layouts: 4.73 us -> none  [on_device(): lax.all_to_all(cost_grad, 'track', split_axis=2, concat_axis=1, tiled=True)]
    all_to_all x1 -> x0, starting transfers between devices: 4.44 us -> none  [on_device(): lax.all_to_all(cost_grad, 'track', split_axis=2, concat_axis=1, tiled=True)]
    convert_element_type x2 -> x0, other arithmetic: 4.18 us -> none  [the longest x1 3.47 us: on_device(): cost_grad = (weights * (grad_x[:, :, None] * coord_x + grad_y[:, :, None]...]
  transfers between devices with their start and end apart: 3 -> 0, of which waited for: 1 -> 0; matrix products, arithmetic and copies ran while one was open for 13% -> 0% of each run, Pallas kernels for 0% -> 0%
where the time goes in v1:
time: 32.4 us; the launch traced here: 32.2 us
  Pallas kernels  25.4 us (78%)
  local copies, waits for them, and re-layouts  6.11 us (19%)
  between operations  0.65 us (2%)
    pallas_call x1, Pallas kernels, on_device(): pl.pallas_call(functools.partial(kernel, n_track, n_frame), out_shape=(ja...  25.4 us
    unnamed x10, local copies, waits for them, and re-layouts  6.11 us

profile of v1, /device:TPU:0, one launch (start us, length us, event | category | flops | bytes accessed | tf_op | source)
XLA Modules:
  0.0 32.2 jit_solution(12415553533172479154)
XLA Ops:
  0.6 0.0 copy-start
  0.6 2.2 %copy-done = bf16[2,4096,256]{2,1,0:T(8,128)(2,1)S(1)} copy-done((bf16[2,4096,256]{2,1,0:T(8,128)(2,1)S(1)}, bf16[2,4096,256]{2,1,0:T(8,128)(2,1)}, u32[]{:S(2)}) %copy-start) | copy-done | bytes 4194328
  2.8 0.0 copy-start.1
  2.8 0.7 %copy-done.1 = f32[2,2,128]{2,1,0:T(2,128)S(1)} copy-done((f32[2,2,128]{2,1,0:T(2,128)S(1)}, f32[2,2,128]{2,1,0:T(2,128)}, u32[]{:S(2)}) %copy-start.1) | copy-done | bytes 2072
  3.5 0.0 copy-start.2
  3.5 0.7 %copy-done.2 = s32[128]{0:T(128)S(1)} copy-done((s32[128]{0:T(128)S(1)}, s32[128]{0:T(128)}, u32[]{:S(2)}) %copy-start.2) | copy-done | bytes 536
  4.2 0.0 copy-start.3
  4.2 0.7 %copy-done.3 = s32[128]{0:T(128)S(1)} copy-done((s32[128]{0:T(128)S(1)}, s32[128]{0:T(128)}, u32[]{:S(2)}) %copy-start.3) | copy-done | bytes 536
  4.8 25.4 %matching_grad.1 = (f32[4096,128]{1,0:T(8,128)S(1)}, f32[32,256]{1,0:T(8,128)S(1)}) custom-call(bf16[2,4096,256]{2,1,0:T(8,128)(2,1)S(1)} %copy-done, s32[1,128]{1,0:T(1,128)S(1)} %bitcast.8, s32[1,128]{1,0:T(1,128)S(1)} %bitcast.9, f32[2,2,128]{2,1,0:T(2,128)S(1)} %copy-done.1), custom_call_target="tpu_custom_call" | custom-call | tf_op jit(solution)/shard_map/matching_grad/pallas_call | solution.py:298
  30.2 1.3 %copy.9 = f32[1024,2,256]{2,1,0:T(2,128)} copy(f32[1024,2,256]{2,1,0:T(2,128)S(1)} %bitcast.7) | data formatting | bytes 4194304
  31.6 0.6 %copy.10 = f32[32,256]{1,0:T(8,128)} copy(f32[32,256]{1,0:T(8,128)S(1)} %get-tuple-element.9) | data formatting | bytes 65536
Async XLA Ops:
  0.6 2.2 %copy-start = (bf16[2,4096,256]{2,1,0:T(8,128)(2,1)S(1)}, bf16[2,4096,256]{2,1,0:T(8,128)(2,1)}, u32[]{:S(2)}) copy-start(bf16[2,4096,256]{2,1,0:T(8,128)(2,1)} %frames_hbm.1) | copy-start | bytes 12582916
  2.8 0.7 %copy-start.1 = (f32[2,2,128]{2,1,0:T(2,128)S(1)}, f32[2,2,128]{2,1,0:T(2,128)}, u32[]{:S(2)}) copy-start(f32[2,2,128]{2,1,0:T(2,128)} %cot_ref.1) | copy-start | bytes 6148
  3.5 0.7 %copy-start.2 = (s32[128]{0:T(128)S(1)}, s32[128]{0:T(128)}, u32[]{:S(2)}) copy-start(s32[128]{0:T(128)} %param.5) | copy-start | bytes 1540
  4.2 0.7 %copy-start.3 = (s32[128]{0:T(128)S(1)}, s32[128]{0:T(128)}, u32[]{:S(2)}) copy-start(s32[128]{0:T(128)} %param.6) | copy-start | bytes 1540

commit v2 on v1

--- a/solution.py
+++ b/solution.py
@@ -27,12 +27,18 @@
     n_track,
     n_frame,
     frames_hbm,
+    query_frame_hbm,
+    query_pixel_hbm,
+    cot_hbm,
+    out_hbm,
+    query_out_ref,
+    fr,
+    out_ref,
+    out_sem,
     query_frame_ref,
     query_pixel_ref,
     cot_ref,
-    out_ref,
-    query_out_ref,
-    fr,
+    small_sem,
     scores,
     picked,
     picked_in,
@@ -69,6 +75,14 @@
     for _, device in track_peers + frame_peers:
         pl.semaphore_signal(barrier, inc=1, device_id=device, device_id_type=MESH)
 
+    small = [
+        pltpu.make_async_copy(src, dst, small_sem.at[i])
+        for i, (src, dst) in enumerate(
+            [(query_frame_hbm, query_frame_ref), (query_pixel_hbm, query_pixel_ref), (cot_hbm, cot_ref)]
+        )
+    ]
+    for load in small:
+        load.start()
     parts = load_sem.shape[1]
     piece = pixels // parts
     loads = []
@@ -87,6 +101,8 @@
     def to_row(column):
         return jnp.sum(jnp.where(eye, column, jnp.zeros_like(column)), axis=0, keepdims=True)
 
+    for load in small:
+        load.wait()
     index = (query_frame_ref[...] - me_f * held) * pixels + query_pixel_ref[...]
     index = to_column(index.astype(jnp.float32)).astype(jnp.int32)
     lane = lax.broadcasted_iota(jnp.int32, (q, piece), 1)
@@ -172,7 +188,7 @@
             scores[t, i] = s
             return functools.reduce(jnp.maximum, split(s), peak)
 
-        peak = lax.fori_loop(0, chunks, score, jnp.full((q, LANES), -jnp.inf, jnp.float32))
+        peak = lax.fori_loop(0, chunks, score, jnp.full((q, LANES), -jnp.inf, jnp.float32), unroll=True)
         peaks.append(jnp.max(peak, axis=1, keepdims=True) * LOG2_SCALE)
 
     columns = []
@@ -192,7 +208,7 @@
             return zero + tail, first + (moment + tail * (i * cols).astype(jnp.float32))
 
         empty = jnp.zeros((q, LANES), jnp.float32)
-        zero, first = lax.fori_loop(0, chunks, expo, (empty, empty))
+        zero, first = lax.fori_loop(0, chunks, expo, (empty, empty), unroll=4)
         mass = jnp.sum(zero, axis=1, keepdims=True)
         mean_x = jnp.sum(zero * lane_x, axis=1, keepdims=True) / mass
         mean_y = jnp.sum(zero * lane_y + first * row_step, axis=1, keepdims=True) / mass
@@ -232,7 +248,7 @@
             grad = (scores[t, i] * jnp.concatenate(at, axis=1)).astype(jnp.bfloat16)
             return total + dot(grad, chunk_of(t, i), ((1,), (0,)))
 
-        total = lax.fori_loop(0, chunks, query_part, total)
+        total = lax.fori_loop(0, chunks, query_part, total, unroll=True)
     term[...] = total.reshape(n_frame, rows, channels)
     term_copies = []
     for d, device in frame_peers:
@@ -254,11 +270,15 @@
     tracks = n_track * q
     everyone = feats[...].reshape(tracks, channels)
     levels = jnp.concatenate([stats[k] for k in range(n_track)], axis=1)
-    size = max(FEAT_W, min(block, 131072 // tracks // FEAT_W * FEAT_W))
+    size = block // out_sem.shape[0]
     lines = size // FEAT_W
     tiles = channels // LANES
     column_x = lax.broadcasted_iota(jnp.int32, (FEAT_W, 1), 0).astype(jnp.float32)
     slopes = [levels[4 * t + 1 : 4 * t + 2] * column_x for t in range(held)]
+
+    def store(i):
+        where = pl.ds(i * (size * tiles * held), size * tiles * held)
+        return pltpu.make_async_copy(out_ref.at[where], out_hbm.at[where], out_sem.at[i])
 
     def frame_part(i, carry):
         start = me_t * block + i * size
@@ -273,15 +293,18 @@
             for c in range(tiles):
                 place = pl.ds(i * (size * tiles * held) + c * held + t, size, stride=tiles * held)
                 out_ref[place, :] = result[:, c * LANES : (c + 1) * LANES]
+        store(i).start()
         return carry
 
-    lax.fori_loop(0, block // size, frame_part, 0)
+    lax.fori_loop(0, block // size, frame_part, 0, unroll=2)
 
     mine = term[me_f]
     for d, copy in enumerate(term_copies, 1):
         copy.wait_recv()
         mine += term_in[d]
     query_out_ref[...] = mine
+    for i in range(block // size):
+        store(i).wait()
     for copy in sends:
         copy.wait_send()
 
@@ -293,6 +316,7 @@
     block = pixels // n_track
     tiles = channels // LANES
     wide = 4 * LANES
+    size = max(FEAT_W, min(block, 131072 // (n_track * q) // FEAT_W * FEAT_W))
     vmem = pl.BlockSpec(memory_space=pltpu.VMEM)
     dma = pltpu.SemaphoreType.DMA
     frame_grad, query_grad = pl.pallas_call(
@@ -301,10 +325,16 @@
             jax.ShapeDtypeStruct((block * tiles * held, LANES), jnp.float32),
             jax.ShapeDtypeStruct((rows, channels), jnp.float32),
         ),
-        in_specs=[pl.BlockSpec(memory_space=pl.ANY), vmem, vmem, vmem],
-        out_specs=(vmem, vmem),
+        in_specs=[pl.BlockSpec(memory_space=pltpu.HBM)] * 4,
+        out_specs=(pl.BlockSpec(memory_space=pltpu.HBM), vmem),
         scratch_shapes=[
             pltpu.VMEM((held, pixels, channels), jnp.bfloat16),
+            pltpu.VMEM((block * tiles * held, LANES), jnp.float32),
+            dma((block // size,)),
+            pltpu.VMEM((1, q), jnp.int32),
+            pltpu.VMEM((1, q), jnp.int32),
+            pltpu.VMEM(cotangent.shape, jnp.float32),
+            dma((3,)),
             pltpu.VMEM((held, pixels // wide, q, wide), jnp.float32),
             pltpu.VMEM((n_frame, rows, channels), jnp.bfloat16),
             pltpu.VMEM((n_frame, rows, channels), jnp.bfloat16),
@@ -325,7 +355,7 @@
             dma((n_frame,)),
         ],
         compiler_params=pltpu.CompilerParams(
-            collective_id=0, has_side_effects=True, vmem_limit_bytes=40 * 2**20
+            collective_id=0, has_side_effects=True, vmem_limit_bytes=64 * 2**20
         ),
         name="matching_grad",
     )(frames, query_frame.reshape(1, q), query_pixel.reshape(1, q), cotangent)

time: 32.4 us -> 29.2 us (0.901)
  local copies, waits for them, and re-layouts: 6.11 us -> 4.25 us
  Pallas kernels: 25.4 us -> 24.1 us
    unnamed x10 -> x4, local copies, waits for them, and re-layouts: 6.11 us -> 4.25 us
    pallas_call x1, Pallas kernels: 25.4 us -> 24.1 us  [on_device(): pl.pallas_call(functools.partial(kernel, n_track, n_frame), out_shape=(ja...]
where the time goes in v2:
time: 29.2 us; the launch traced here: 29 us
  Pallas kernels  24.1 us (83%)
  local copies, waits for them, and re-layouts  4.25 us (15%)
  between operations  0.65 us (2%)
    pallas_call x1, Pallas kernels, on_device(): pl.pallas_call(functools.partial(kernel, n_track, n_frame), out_shape=(ja...  24.1 us
    unnamed x4, local copies, waits for them, and re-layouts  4.25 us

profile of v2, /device:TPU:0, one launch (start us, length us, event | category | flops | bytes accessed | tf_op | source)
XLA Modules:
  0.0 29.0 jit_solution(13595117370340374965)
XLA Ops:
  0.6 24.1 %matching_grad.1 = (f32[4096,128]{1,0:T(8,128)}, f32[32,256]{1,0:T(8,128)}) custom-call(bf16[2,4096,256]{2,1,0:T(8,128)(2,1)} %frames_hbm.1, s32[1,128]{1,0:T(1,128)} %bitcast.8, s32[1,128]{1,0:T(1,128)} %bitcast.9, f32[2,2,128]{2,1,0:T(2,128)} %cot_hbm.1), custom_call_target="tpu_custom_call" | custom-call | tf_op jit(solution)/shard_map/matching_grad/pallas_call | solution.py:322
  24.8 0.0 copy-start
  24.8 3.6 %copy.9 = f32[1024,2,256]{2,1,0:T(2,128)} copy(f32[1024,2,256]{2,1,0:T(2,128)} %bitcast.7) | data formatting | bytes 4194304
  28.4 0.0 copy-done
  28.4 0.6 %copy.10 = f32[32,256]{1,0:T(8,128)} copy(f32[32,256]{1,0:T(8,128)S(1)} %copy-done) | data formatting | bytes 65536
Async XLA Ops:
  24.8 3.6 %copy-start = (f32[32,256]{1,0:T(8,128)S(1)}, f32[32,256]{1,0:T(8,128)}, u32[]{:S(2)}) copy-start(f32[32,256]{1,0:T(8,128)} %get-tuple-element.9) | copy-start | bytes 98308

commit v3 on v1

--- a/solution.py
+++ b/solution.py
@@ -1,5 +1,4 @@
 import functools
-import math
 
 import jax
 import jax.numpy as jnp
@@ -14,7 +13,6 @@
 LANES = 128
 MESH = pl.DeviceIdType.MESH
 SCORE_SCALE = C ** (-0.5)
-LOG2_SCALE = SCORE_SCALE * math.log2(math.e)
 STEP_X = 2.0 / (FEAT_W - 1)
 STEP_Y = 2.0 / (FEAT_H - 1)
 
@@ -27,9 +25,7 @@
     n_track,
     n_frame,
     frames_hbm,
-    query_frame_ref,
-    query_pixel_ref,
-    cot_ref,
+    small_ref,
     out_ref,
     query_out_ref,
     fr,
@@ -53,7 +49,7 @@
     term_recv,
 ):
     held, pixels, channels = fr.shape
-    q = cot_ref.shape[2]
+    q = small_ref.shape[1]
     rows = q // n_frame
     block = pixels // n_track
     me_t = lax.axis_index("track")
@@ -87,7 +83,8 @@
     def to_row(column):
         return jnp.sum(jnp.where(eye, column, jnp.zeros_like(column)), axis=0, keepdims=True)
 
-    index = (query_frame_ref[...] - me_f * held) * pixels + query_pixel_ref[...]
+    index = (small_ref[2 * held : 2 * held + 1, :].astype(jnp.int32) - me_f * held) * pixels
+    index += small_ref[2 * held + 1 : 2 * held + 2, :].astype(jnp.int32)
     index = to_column(index.astype(jnp.float32)).astype(jnp.int32)
     lane = lax.broadcasted_iota(jnp.int32, (q, piece), 1)
     total = jnp.zeros((q, channels), jnp.float32)
@@ -164,75 +161,77 @@
     def chunk_of(t, i):
         return fr[t, pl.ds(pl.multiple_of(i * wide, wide), wide), :]
 
-    peaks = []
-    for t in range(held):
-
-        def score(i, peak):
-            s = dot(own, chunk_of(t, i), ((1,), (1,)))
-            scores[t, i] = s
-            return functools.reduce(jnp.maximum, split(s), peak)
-
-        peak = lax.fori_loop(0, chunks, score, jnp.full((q, LANES), -jnp.inf, jnp.float32))
-        peaks.append(jnp.max(peak, axis=1, keepdims=True) * LOG2_SCALE)
-
-    columns = []
-    for t in range(held):
-
-        def expo(i, carry):
-            zero, first = carry
-            e = jnp.exp2(scores[t, i] * LOG2_SCALE - peaks[t])
-            scores[t, i] = e
-            e = split(e)
-            tail = e[-1]
-            moment = tail
-            for part in e[-2:0:-1]:
-                tail = tail + part
-                moment = moment + tail
-            tail = tail + e[0]
-            return zero + tail, first + (moment + tail * (i * cols).astype(jnp.float32))
-
-        empty = jnp.zeros((q, LANES), jnp.float32)
-        zero, first = lax.fori_loop(0, chunks, expo, (empty, empty))
+    def scores_step(t, i, peak):
+        s = dot(own, chunk_of(t, i), ((1,), (1,)))
+        scores[t, i] = s
+        return functools.reduce(jnp.maximum, split(s), peak)
+
+    def expo_step(t, i, carry):
+        zero, first = carry
+        e = jnp.exp(scores[t, i] * SCORE_SCALE - peaks[t])
+        scores[t, i] = e
+        e = split(e)
+        tail = e[-1]
+        moment = tail
+        for part in e[-2:0:-1]:
+            tail = tail + part
+            moment = moment + tail
+        tail = tail + e[0]
+        return zero + tail, first + (moment + tail * float(i * cols))
+
+    def query_step(t, i, total):
+        slope_x, slope_y, level = columns[t]
+        base = level + slope_x * lane_x + slope_y * lane_y
+        at = [base + slope_y * float((i * cols + c) * row_step) for c in range(cols)]
+        grad = (scores[t, i] * jnp.concatenate(at, axis=1)).astype(jnp.bfloat16)
+        return total + dot(grad, chunk_of(t, i), ((1,), (0,)))
+
+    def softmax_terms(t, zero, first):
         mass = jnp.sum(zero, axis=1, keepdims=True)
         mean_x = jnp.sum(zero * lane_x, axis=1, keepdims=True) / mass
         mean_y = jnp.sum(zero * lane_y + first * row_step, axis=1, keepdims=True) / mass
-        grad_x = to_column(cot_ref[0, t : t + 1, :])
-        grad_y = to_column(cot_ref[1, t : t + 1, :])
+        grad_x = to_column(small_ref[t : t + 1, :])
+        grad_y = to_column(small_ref[held + t : held + t + 1, :])
         scale = SCORE_SCALE / mass
         slope_x = grad_x * STEP_X * scale
         slope_y = grad_y * STEP_Y * scale
-        columns.append((slope_x, slope_y, -(slope_x * mean_x + slope_y * mean_y)))
-
-    for t in range(held):
-        for i, column in enumerate((peaks[t],) + columns[t]):
-            stats[me_t, 4 * t + i : 4 * t + i + 1, :] = to_row(column)
-    stat_copies = []
-    for d, device in track_peers:
-        stat_copies.append(
-            pltpu.make_async_remote_copy(
-                src_ref=stats.at[me_t],
-                dst_ref=stats.at[me_t],
-                send_sem=stat_send.at[d],
-                recv_sem=stat_recv.at[d],
-                device_id=device,
-                device_id_type=MESH,
-            )
-        )
-        stat_copies[-1].start()
+        return slope_x, slope_y, -(slope_x * mean_x + slope_y * mean_y)
+
+    peaks, columns, stat_copies = {}, {}, []
+    total = jnp.zeros((q, channels), jnp.float32)
+    empty = jnp.zeros((q, LANES), jnp.float32)
+    for turn in range(held + 2):
+        peak = jnp.full((q, LANES), -jnp.inf, jnp.float32)
+        sums = (empty, empty)
+        for i in range(chunks):
+            if turn < held:
+                peak = scores_step(turn, i, peak)
+            if 0 <= turn - 1 < held:
+                sums = expo_step(turn - 1, i, sums)
+            if 0 <= turn - 2 < held:
+                total = query_step(turn - 2, i, total)
+        if turn < held:
+            peaks[turn] = jnp.max(peak, axis=1, keepdims=True) * SCORE_SCALE
+        if 0 <= turn - 1 < held:
+            columns[turn - 1] = softmax_terms(turn - 1, *sums)
+        if turn == held:
+            for t in range(held):
+                for i, column in enumerate((peaks[t],) + columns[t]):
+                    stats[me_t, 4 * t + i : 4 * t + i + 1, :] = to_row(column)
+            for d, device in track_peers:
+                stat_copies.append(
+                    pltpu.make_async_remote_copy(
+                        src_ref=stats.at[me_t],
+                        dst_ref=stats.at[me_t],
+                        send_sem=stat_send.at[d],
+                        recv_sem=stat_recv.at[d],
+                        device_id=device,
+                        device_id_type=MESH,
+                    )
+                )
+                stat_copies[-1].start()
     sends += stat_copies
 
-    total = jnp.zeros((q, channels), jnp.float32)
-    for t in range(held):
-        slope_x, slope_y, level = columns[t]
-        base = level + slope_x * lane_x + slope_y * lane_y
-        step = slope_y * row_step
-
-        def query_part(i, total):
-            at = [base + step * (i * cols + c).astype(jnp.float32) for c in range(cols)]
-            grad = (scores[t, i] * jnp.concatenate(at, axis=1)).astype(jnp.bfloat16)
-            return total + dot(grad, chunk_of(t, i), ((1,), (0,)))
-
-        total = lax.fori_loop(0, chunks, query_part, total)
     term[...] = total.reshape(n_frame, rows, channels)
     term_copies = []
     for d, device in frame_peers:
@@ -266,7 +265,7 @@
         for t in range(held):
             peak, _, slope_y, level = [levels[4 * t + j : 4 * t + j + 1] for j in range(4)]
             s = dot(fr[t, pl.ds(pl.multiple_of(start, FEAT_W), size), :], everyone, ((1,), (1,)))
-            e = jnp.exp2(s * LOG2_SCALE - peak)
+            e = jnp.exp(s * SCORE_SCALE - peak)
             at = [slopes[t] + (level + slope_y * (first_line + l).astype(jnp.float32)) for l in range(lines)]
             grad = (e * jnp.concatenate(at, axis=0)).astype(jnp.bfloat16)
             result = dot(grad, everyone, ((1,), (0,)))
@@ -275,7 +274,7 @@
                 out_ref[place, :] = result[:, c * LANES : (c + 1) * LANES]
         return carry
 
-    lax.fori_loop(0, block // size, frame_part, 0)
+    lax.fori_loop(0, block // size, frame_part, 0, unroll=True)
 
     mine = term[me_f]
     for d, copy in enumerate(term_copies, 1):
@@ -293,6 +292,10 @@
     block = pixels // n_track
     tiles = channels // LANES
     wide = 4 * LANES
+    line = lax.broadcasted_iota(jnp.int32, (2 * held + 2, q), 0)
+    small = jnp.pad(cotangent.reshape(2 * held, q), ((0, 2), (0, 0)))
+    small = jnp.where(line == 2 * held, query_frame.astype(jnp.float32), small)
+    small = jnp.where(line == 2 * held + 1, query_pixel.astype(jnp.float32), small)
     vmem = pl.BlockSpec(memory_space=pltpu.VMEM)
     dma = pltpu.SemaphoreType.DMA
     frame_grad, query_grad = pl.pallas_call(
@@ -301,7 +304,7 @@
             jax.ShapeDtypeStruct((block * tiles * held, LANES), jnp.float32),
             jax.ShapeDtypeStruct((rows, channels), jnp.float32),
         ),
-        in_specs=[pl.BlockSpec(memory_space=pl.ANY), vmem, vmem, vmem],
+        in_specs=[pl.BlockSpec(memory_space=pltpu.HBM), vmem],
         out_specs=(vmem, vmem),
         scratch_shapes=[
             pltpu.VMEM((held, pixels, channels), jnp.bfloat16),
@@ -325,10 +328,10 @@
             dma((n_frame,)),
         ],
         compiler_params=pltpu.CompilerParams(
-            collective_id=0, has_side_effects=True, vmem_limit_bytes=40 * 2**20
+            collective_id=0, has_side_effects=True, vmem_limit_bytes=60 * 2**20
         ),
         name="matching_grad",
-    )(frames, query_frame.reshape(1, q), query_pixel.reshape(1, q), cotangent)
+    )(frames, small)
     frame_grad = frame_grad.reshape(block, tiles, held, LANES).transpose(0, 2, 1, 3)
     return (frame_grad.reshape(block, held, channels), query_grad)
 

time: 32.4 us -> 31.4 us (0.969)
  other arithmetic: 0 us -> 2.67 us
  local copies, waits for them, and re-layouts: 6.11 us -> 4.25 us
  Pallas kernels: 25.4 us -> 23.6 us
    pallas_call x1, Pallas kernels: 25.4 us -> 23.6 us  [on_device(): pl.pallas_call(functools.partial(kernel, n_track, n_frame), out_shape=(ja...]
    unnamed x10 -> x4, local copies, waits for them, and re-layouts: 6.11 us -> 4.25 us
    select_n x0 -> x1, other arithmetic: none -> 1.35 us  [on_device(): jnp.where(line == 2 * held + 1, query_pixel.astype(jnp.float32), small)]
    convert_element_type x0 -> x2, other arithmetic: none -> 1.32 us  [the longest x1 0.66 us: on_device(): small = jnp.where(line == 2 * held, query_frame.astype(jnp.float32), small)]
where the time goes in v3:
time: 31.4 us; the launch traced here: 31.1 us
  Pallas kernels  23.6 us (75%)
  local copies, waits for them, and re-layouts  4.25 us (14%)
  other arithmetic  2.67 us (9%)
  between operations  0.65 us (2%)
    pallas_call x1, Pallas kernels, on_device(): pl.pallas_call(functools.partial(kernel, n_track, n_frame), out_shape=(ja...  23.6 us
    unnamed x4, local copies, waits for them, and re-layouts  4.25 us
    select_n x1, other arithmetic, on_device(): jnp.where(line == 2 * held + 1, query_pixel.astype(jnp.float32), small)  1.35 us
    convert_element_type x1, other arithmetic, on_device(): small = jnp.where(line == 2 * held, query_frame.astype(jnp.float32), small)  0.66 us
    convert_element_type x1, other arithmetic, on_device(): query_pixel.astype(jnp.float32)  0.66 us

profile of v3, /device:TPU:0, one launch (start us, length us, event | category | flops | bytes accessed | tf_op | source)
XLA Modules:
  0.0 31.1 jit_solution(14300978994809733661)
XLA Ops:
  0.6 0.7 %convert_element_type.9 = f32[128]{0:T(128)S(1)} convert(s32[128]{0:T(128)} %param.5) | non-fusion elementwise | flops 128 | bytes 1024 | tf_op jit(solution)/shard_map/convert_element_type | solution.py:297
  1.3 0.7 %convert_element_type.8 = f32[128]{0:T(128)S(1)} convert(s32[128]{0:T(128)} %param.6) | non-fusion elementwise | flops 128 | bytes 1024 | tf_op jit(solution)/shard_map/convert_element_type | solution.py:298
  2.0 1.3 %select_select_fusion.small_ref = f32[6,128]{1,0:T(8,128)} fusion(f32[4,128]{1,0:T(4,128)} %bitcast.7, f32[128]{0:T(128)S(1)} %convert_element_type.9, f32[128]{0:T(128)S(1)} %convert_element_type.8, pred[6]{0:T(512)(128)(4,1)S(1)} %get-tuple-element.6, pred[6]{0:T(512)(128)(4,1)S(1)} %get-tuple-element.7), kind=kLoop, calls=%fused_computation | loop fusion | flops 1536 | bytes 6156 | tf_op jit(solution)/shard_map/jit(_where)/select_n | solution.py:298
  3.3 23.6 %matching_grad.1 = (f32[4096,128]{1,0:T(8,128)}, f32[32,256]{1,0:T(8,128)}) custom-call(bf16[2,4096,256]{2,1,0:T(8,128)(2,1)} %frames_hbm.1, f32[6,128]{1,0:T(8,128)} %select_select_fusion.small_ref), custom_call_target="tpu_custom_call" | custom-call | tf_op jit(solution)/shard_map/matching_grad/pallas_call | solution.py:301
  26.9 0.0 copy-start
  26.9 3.6 %copy.9 = f32[1024,2,256]{2,1,0:T(2,128)} copy(f32[1024,2,256]{2,1,0:T(2,128)} %bitcast.6) | data formatting | bytes 4194304
  30.5 0.0 copy-done
  30.5 0.6 %copy.10 = f32[32,256]{1,0:T(8,128)} copy(f32[32,256]{1,0:T(8,128)S(1)} %copy-done) | data formatting | bytes 65536
  (1 shorter events, 0.0 us)
Async XLA Ops:
  26.9 3.6 %copy-start = (f32[32,256]{1,0:T(8,128)S(1)}, f32[32,256]{1,0:T(8,128)}, u32[]{:S(2)}) copy-start(f32[32,256]{1,0:T(8,128)} %get-tuple-element.11) | copy-start | bytes 98308

commit v4 on v3

--- a/solution.py
+++ b/solution.py
@@ -25,7 +25,8 @@
     n_track,
     n_frame,
     frames_hbm,
-    small_ref,
+    index_ref,
+    cot_ref,
     out_ref,
     query_out_ref,
     fr,
@@ -49,7 +50,7 @@
     term_recv,
 ):
     held, pixels, channels = fr.shape
-    q = small_ref.shape[1]
+    q = index_ref.shape[1]
     rows = q // n_frame
     block = pixels // n_track
     me_t = lax.axis_index("track")
@@ -83,9 +84,7 @@
     def to_row(column):
         return jnp.sum(jnp.where(eye, column, jnp.zeros_like(column)), axis=0, keepdims=True)
 
-    index = (small_ref[2 * held : 2 * held + 1, :].astype(jnp.int32) - me_f * held) * pixels
-    index += small_ref[2 * held + 1 : 2 * held + 2, :].astype(jnp.int32)
-    index = to_column(index.astype(jnp.float32)).astype(jnp.int32)
+    index = to_column(index_ref[...]).astype(jnp.int32) - me_f * (held * pixels)
     lane = lax.broadcasted_iota(jnp.int32, (q, piece), 1)
     total = jnp.zeros((q, channels), jnp.float32)
     for t, i, load in loads:
@@ -146,7 +145,7 @@
         feat_copies[-1].start()
     sends += feat_copies
 
-    own = feats[me_t].reshape(q, channels)
+    own = feats[me_t].reshape(q, channels) * jnp.bfloat16(SCORE_SCALE)
     wide = scores.shape[3]
     cols = wide // LANES
     chunks = pixels // wide
@@ -168,9 +167,8 @@
 
     def expo_step(t, i, carry):
         zero, first = carry
-        e = jnp.exp(scores[t, i] * SCORE_SCALE - peaks[t])
-        scores[t, i] = e
-        e = split(e)
+        e = [jnp.exp(part - wide_peaks[t]) for part in split(scores[t, i])]
+        scores[t, i] = jnp.concatenate(e, axis=1)
         tail = e[-1]
         moment = tail
         for part in e[-2:0:-1]:
@@ -180,24 +178,25 @@
         return zero + tail, first + (moment + tail * float(i * cols))
 
     def query_step(t, i, total):
-        slope_x, slope_y, level = columns[t]
-        base = level + slope_x * lane_x + slope_y * lane_y
-        at = [base + slope_y * float((i * cols + c) * row_step) for c in range(cols)]
-        grad = (scores[t, i] * jnp.concatenate(at, axis=1)).astype(jnp.bfloat16)
-        return total + dot(grad, chunk_of(t, i), ((1,), (0,)))
+        base, step = lines_of[t]
+        grad = [
+            (part * (base + step * float(i * cols + c))).astype(jnp.bfloat16)
+            for c, part in enumerate(split(scores[t, i]))
+        ]
+        return total + dot(jnp.concatenate(grad, axis=1), chunk_of(t, i), ((1,), (0,)))
 
     def softmax_terms(t, zero, first):
         mass = jnp.sum(zero, axis=1, keepdims=True)
         mean_x = jnp.sum(zero * lane_x, axis=1, keepdims=True) / mass
         mean_y = jnp.sum(zero * lane_y + first * row_step, axis=1, keepdims=True) / mass
-        grad_x = to_column(small_ref[t : t + 1, :])
-        grad_y = to_column(small_ref[held + t : held + t + 1, :])
+        grad_x = to_column(cot_ref[0, t : t + 1, :])
+        grad_y = to_column(cot_ref[1, t : t + 1, :])
         scale = SCORE_SCALE / mass
         slope_x = grad_x * STEP_X * scale
         slope_y = grad_y * STEP_Y * scale
         return slope_x, slope_y, -(slope_x * mean_x + slope_y * mean_y)
 
-    peaks, columns, stat_copies = {}, {}, []
+    peaks, wide_peaks, columns, lines_of, stat_copies = {}, {}, {}, {}, []
     total = jnp.zeros((q, channels), jnp.float32)
     empty = jnp.zeros((q, LANES), jnp.float32)
     for turn in range(held + 2):
@@ -211,9 +210,12 @@
             if 0 <= turn - 2 < held:
                 total = query_step(turn - 2, i, total)
         if turn < held:
-            peaks[turn] = jnp.max(peak, axis=1, keepdims=True) * SCORE_SCALE
+            peaks[turn] = jnp.max(peak, axis=1, keepdims=True)
+            wide_peaks[turn] = jnp.broadcast_to(peaks[turn], (q, LANES))
         if 0 <= turn - 1 < held:
-            columns[turn - 1] = softmax_terms(turn - 1, *sums)
+            slope_x, slope_y, level = columns[turn - 1] = softmax_terms(turn - 1, *sums)
+            step = jnp.broadcast_to(slope_y, (q, LANES))
+            lines_of[turn - 1] = (level + slope_x * lane_x + step * lane_y, step * row_step)
         if turn == held:
             for t in range(held):
                 for i, column in enumerate((peaks[t],) + columns[t]):
@@ -252,6 +254,7 @@
         copy.wait_recv()
     tracks = n_track * q
     everyone = feats[...].reshape(tracks, channels)
+    scaled = everyone * jnp.bfloat16(SCORE_SCALE)
     levels = jnp.concatenate([stats[k] for k in range(n_track)], axis=1)
     size = max(FEAT_W, min(block, 131072 // tracks // FEAT_W * FEAT_W))
     lines = size // FEAT_W
@@ -264,8 +267,8 @@
         first_line = me_t * (block // FEAT_W) + i * lines
         for t in range(held):
             peak, _, slope_y, level = [levels[4 * t + j : 4 * t + j + 1] for j in range(4)]
-            s = dot(fr[t, pl.ds(pl.multiple_of(start, FEAT_W), size), :], everyone, ((1,), (1,)))
-            e = jnp.exp(s * SCORE_SCALE - peak)
+            s = dot(fr[t, pl.ds(pl.multiple_of(start, FEAT_W), size), :], scaled, ((1,), (1,)))
+            e = jnp.exp(s - peak)
             at = [slopes[t] + (level + slope_y * (first_line + l).astype(jnp.float32)) for l in range(lines)]
             grad = (e * jnp.concatenate(at, axis=0)).astype(jnp.bfloat16)
             result = dot(grad, everyone, ((1,), (0,)))
@@ -292,10 +295,7 @@
     block = pixels // n_track
     tiles = channels // LANES
     wide = 4 * LANES
-    line = lax.broadcasted_iota(jnp.int32, (2 * held + 2, q), 0)
-    small = jnp.pad(cotangent.reshape(2 * held, q), ((0, 2), (0, 0)))
-    small = jnp.where(line == 2 * held, query_frame.astype(jnp.float32), small)
-    small = jnp.where(line == 2 * held + 1, query_pixel.astype(jnp.float32), small)
+    index = (query_frame * pixels + query_pixel).astype(jnp.float32).reshape(1, q)
     vmem = pl.BlockSpec(memory_space=pltpu.VMEM)
     dma = pltpu.SemaphoreType.DMA
     frame_grad, query_grad = pl.pallas_call(
@@ -304,7 +304,7 @@
             jax.ShapeDtypeStruct((block * tiles * held, LANES), jnp.float32),
             jax.ShapeDtypeStruct((rows, channels), jnp.float32),
         ),
-        in_specs=[pl.BlockSpec(memory_space=pltpu.HBM), vmem],
+        in_specs=[pl.BlockSpec(memory_space=pltpu.HBM), vmem, vmem],
         out_specs=(vmem, vmem),
         scratch_shapes=[
             pltpu.VMEM((held, pixels, channels), jnp.bfloat16),
@@ -328,10 +328,10 @@
             dma((n_frame,)),
         ],
         compiler_params=pltpu.CompilerParams(
-            collective_id=0, has_side_effects=True, vmem_limit_bytes=60 * 2**20
+            collective_id=0, has_side_effects=True, vmem_limit_bytes=56 * 2**20
         ),
         name="matching_grad",
-    )(frames, small)
+    )(frames, index, cotangent)
     frame_grad = frame_grad.reshape(block, tiles, held, LANES).transpose(0, 2, 1, 3)
     return (frame_grad.reshape(block, held, channels), query_grad)
 

time: 31.4 us -> 29.5 us (0.939)
  other arithmetic: 2.67 us -> 1.19 us
  Pallas kernels: 23.6 us -> 23.2 us
    select_n x1 -> x0, other arithmetic: 1.35 us -> none  [on_device(): jnp.where(line == 2 * held + 1, query_pixel.astype(jnp.float32), small)]
    convert_element_type x2 -> x0, other arithmetic: 1.32 us -> none  [the longest x1 0.66 us: on_device(): small = jnp.where(line == 2 * held, query_frame.astype(jnp.float32), small)]
    reshape x0 -> x1, other arithmetic: none -> 1.19 us  [on_device(): (query_frame * pixels + query_pixel).astype(jnp.float32).reshape(1, q)]
    pallas_call x1, Pallas kernels: 23.6 us -> 23.2 us  [on_device(): pl.pallas_call(functools.partial(kernel, n_track, n_frame), out_shape=(ja...]
where the time goes in v4:
time: 29.5 us; the launch traced here: 29.3 us
  Pallas kernels  23.2 us (79%)
  local copies, waits for them, and re-layouts  4.25 us (14%)
  other arithmetic  1.19 us (4%)
  between operations  0.65 us (2%)
    pallas_call x1, Pallas kernels, on_device(): pl.pallas_call(functools.partial(kernel, n_track, n_frame), out_shape=(ja...  23.2 us
    unnamed x4, local copies, waits for them, and re-layouts  4.25 us
    reshape x1, other arithmetic, on_device(): (query_frame * pixels + query_pixel).astype(jnp.float32).reshape(1, q)  1.19 us

profile of v4, /device:TPU:0, one launch (start us, length us, event | category | flops | bytes accessed | tf_op | source)
XLA Modules:
  0.0 29.3 jit_solution(15527791048738606555)
XLA Ops:
  0.6 1.2 %convert_bitcast_fusion.index_ref = f32[1,128]{1,0:T(1,128)} fusion(s32[128]{0:T(128)} %param.6, s32[128]{0:T(128)} %param.5), kind=kLoop, calls=%fused_computation | loop fusion | flops 384 | bytes 1536 | tf_op jit(solution)/shard_map/reshape | solution.py:298
  1.8 23.2 %matching_grad.1 = (f32[4096,128]{1,0:T(8,128)}, f32[32,256]{1,0:T(8,128)}) custom-call(bf16[2,4096,256]{2,1,0:T(8,128)(2,1)} %frames_hbm.1, f32[1,128]{1,0:T(1,128)} %convert_bitcast_fusion.index_ref, f32[2,2,128]{2,1,0:T(2,128)} %cot_ref.1), custom_call_target="tpu_custom_call" | custom-call | tf_op jit(solution)/shard_map/matching_grad/pallas_call | solution.py:301
  25.1 0.0 copy-start
  25.1 3.6 %copy.9 = f32[1024,2,256]{2,1,0:T(2,128)} copy(f32[1024,2,256]{2,1,0:T(2,128)} %bitcast.7) | data formatting | bytes 4194304
  28.7 0.0 copy-done
  28.7 0.6 %copy.10 = f32[32,256]{1,0:T(8,128)} copy(f32[32,256]{1,0:T(8,128)S(1)} %copy-done) | data formatting | bytes 65536
Async XLA Ops:
  25.1 3.6 %copy-start = (f32[32,256]{1,0:T(8,128)S(1)}, f32[32,256]{1,0:T(8,128)}, u32[]{:S(2)}) copy-start(f32[32,256]{1,0:T(8,128)} %get-tuple-element.9) | copy-start | bytes 98308

commit v5 on v4

--- a/solution.py
+++ b/solution.py
@@ -328,7 +328,7 @@
             dma((n_frame,)),
         ],
         compiler_params=pltpu.CompilerParams(
-            collective_id=0, has_side_effects=True, vmem_limit_bytes=56 * 2**20
+            collective_id=0, has_side_effects=True, vmem_limit_bytes=48 * 2**20
         ),
         name="matching_grad",
     )(frames, index, cotangent)

time: 29.5 us -> 25.3 us (0.86)
  Pallas kernels: 23.2 us -> 21.2 us
  local copies, waits for them, and re-layouts: 4.25 us -> 2.62 us
  other arithmetic: 1.19 us -> 0.68 us
    pallas_call x1, Pallas kernels: 23.2 us -> 21.2 us  [on_device(): pl.pallas_call(functools.partial(kernel, n_track, n_frame), out_shape=(ja...]
    unnamed x4, local copies, waits for them, and re-layouts: 4.25 us -> 2.62 us
    reshape x1, other arithmetic: 1.19 us -> 0.68 us  [on_device(): (query_frame * pixels + query_pixel).astype(jnp.float32).reshape(1, q)]
where the time goes in v5:
time: 25.3 us; the launch traced here: 25.1 us
  Pallas kernels  21.2 us (84%)
  local copies, waits for them, and re-layouts  2.62 us (10%)
  other arithmetic  0.68 us (3%)
  between operations  0.64 us (3%)
    pallas_call x1, Pallas kernels, on_device(): pl.pallas_call(functools.partial(kernel, n_track, n_frame), out_shape=(ja...  21.2 us
    unnamed x4, local copies, waits for them, and re-layouts  2.62 us
    reshape x1, other arithmetic, on_device(): (query_frame * pixels + query_pixel).astype(jnp.float32).reshape(1, q)  0.68 us

profile of v5, /device:TPU:0, one launch (start us, length us, event | category | flops | bytes accessed | tf_op | source)
XLA Modules:
  0.0 25.1 jit_solution(11806020176574093485)
XLA Ops:
  0.6 0.7 %convert_bitcast_fusion.index_ref = f32[1,128]{1,0:T(1,128)S(1)} fusion(s32[128]{0:T(128)} %param.6, s32[128]{0:T(128)} %param.5), kind=kLoop, calls=%fused_computation | loop fusion | flops 384 | bytes 1536 | tf_op jit(solution)/shard_map/reshape | solution.py:298
  1.3 0.0 copy-start
  1.3 0.7 %copy-done = f32[2,2,128]{2,1,0:T(2,128)S(1)} copy-done((f32[2,2,128]{2,1,0:T(2,128)S(1)}, f32[2,2,128]{2,1,0:T(2,128)}, u32[]{:S(2)}) %copy-start) | copy-done | bytes 2072
  2.0 21.2 %matching_grad.1 = (f32[4096,128]{1,0:T(8,128)S(1)}, f32[32,256]{1,0:T(8,128)S(1)}) custom-call(bf16[2,4096,256]{2,1,0:T(8,128)(2,1)} %frames_hbm.1, f32[1,128]{1,0:T(1,128)S(1)} %convert_bitcast_fusion.index_ref, f32[2,2,128]{2,1,0:T(2,128)S(1)} %copy-done), custom_call_target="tpu_custom_call" | custom-call | tf_op jit(solution)/shard_map/matching_grad/pallas_call | solution.py:301
  23.2 1.3 %copy.9 = f32[1024,2,256]{2,1,0:T(2,128)} copy(f32[1024,2,256]{2,1,0:T(2,128)S(1)} %bitcast.7) | data formatting | bytes 4194304
  24.5 0.6 %copy.10 = f32[32,256]{1,0:T(8,128)} copy(f32[32,256]{1,0:T(8,128)S(1)} %get-tuple-element.9) | data formatting | bytes 65536
Async XLA Ops:
  1.3 0.7 %copy-start = (f32[2,2,128]{2,1,0:T(2,128)S(1)}, f32[2,2,128]{2,1,0:T(2,128)}, u32[]{:S(2)}) copy-start(f32[2,2,128]{2,1,0:T(2,128)} %cot_ref.1) | copy-start | bytes 6148

commit v6 on v5

--- a/solution.py
+++ b/solution.py
@@ -216,22 +216,19 @@
             slope_x, slope_y, level = columns[turn - 1] = softmax_terms(turn - 1, *sums)
             step = jnp.broadcast_to(slope_y, (q, LANES))
             lines_of[turn - 1] = (level + slope_x * lane_x + step * lane_y, step * row_step)
-        if turn == held:
-            for t in range(held):
-                for i, column in enumerate((peaks[t],) + columns[t]):
-                    stats[me_t, 4 * t + i : 4 * t + i + 1, :] = to_row(column)
+            rest = [to_row(column) for column in (peaks[turn - 1],) + columns[turn - 1]]
+            stats[turn - 1, me_t] = jnp.concatenate(rest + rest, axis=0)
             for d, device in track_peers:
-                stat_copies.append(
-                    pltpu.make_async_remote_copy(
-                        src_ref=stats.at[me_t],
-                        dst_ref=stats.at[me_t],
-                        send_sem=stat_send.at[d],
-                        recv_sem=stat_recv.at[d],
-                        device_id=device,
-                        device_id_type=MESH,
-                    )
+                copy = pltpu.make_async_remote_copy(
+                    src_ref=stats.at[turn - 1, me_t],
+                    dst_ref=stats.at[turn - 1, me_t],
+                    send_sem=stat_send.at[turn - 1, d],
+                    recv_sem=stat_recv.at[turn - 1, d],
+                    device_id=device,
+                    device_id_type=MESH,
                 )
-                stat_copies[-1].start()
+                copy.start()
+                stat_copies.append(copy)
     sends += stat_copies
 
     term[...] = total.reshape(n_frame, rows, channels)
@@ -250,34 +247,37 @@
         term_copies[-1].start()
     sends += term_copies
 
-    for copy in feat_copies + stat_copies:
+    for copy in feat_copies:
         copy.wait_recv()
     tracks = n_track * q
     everyone = feats[...].reshape(tracks, channels)
     scaled = everyone * jnp.bfloat16(SCORE_SCALE)
-    levels = jnp.concatenate([stats[k] for k in range(n_track)], axis=1)
     size = max(FEAT_W, min(block, 131072 // tracks // FEAT_W * FEAT_W))
     lines = size // FEAT_W
     tiles = channels // LANES
     column_x = lax.broadcasted_iota(jnp.int32, (FEAT_W, 1), 0).astype(jnp.float32)
-    slopes = [levels[4 * t + 1 : 4 * t + 2] * column_x for t in range(held)]
-
-    def frame_part(i, carry):
-        start = me_t * block + i * size
-        first_line = me_t * (block // FEAT_W) + i * lines
-        for t in range(held):
-            peak, _, slope_y, level = [levels[4 * t + j : 4 * t + j + 1] for j in range(4)]
+
+    for t in range(held):
+        for copy in stat_copies[t * (n_track - 1) : (t + 1) * (n_track - 1)]:
+            copy.wait_recv()
+        levels = jnp.concatenate([stats[t, k] for k in range(n_track)], axis=1)
+        peak, slope_x, slope_y, level = [levels[j : j + 1] for j in range(4)]
+        slope_x = slope_x * column_x
+
+        def frame_part(i, carry):
+            start = me_t * block + i * size
+            first_line = me_t * (block // FEAT_W) + i * lines
             s = dot(fr[t, pl.ds(pl.multiple_of(start, FEAT_W), size), :], scaled, ((1,), (1,)))
             e = jnp.exp(s - peak)
-            at = [slopes[t] + (level + slope_y * (first_line + l).astype(jnp.float32)) for l in range(lines)]
+            at = [slope_x + (level + slope_y * (first_line + l).astype(jnp.float32)) for l in range(lines)]
             grad = (e * jnp.concatenate(at, axis=0)).astype(jnp.bfloat16)
             result = dot(grad, everyone, ((1,), (0,)))
             for c in range(tiles):
                 place = pl.ds(i * (size * tiles * held) + c * held + t, size, stride=tiles * held)
                 out_ref[place, :] = result[:, c * LANES : (c + 1) * LANES]
-        return carry
-
-    lax.fori_loop(0, block // size, frame_part, 0, unroll=True)
+            return carry
+
+        lax.fori_loop(0, block // size, frame_part, 0, unroll=True)
 
     mine = term[me_f]
     for d, copy in enumerate(term_copies, 1):
@@ -312,7 +312,7 @@
             pltpu.VMEM((n_frame, rows, channels), jnp.bfloat16),
             pltpu.VMEM((n_frame, rows, channels), jnp.bfloat16),
             pltpu.VMEM((n_track, n_frame, rows, channels), jnp.bfloat16),
-            pltpu.VMEM((n_track, 4 * held, q), jnp.float32),
+            pltpu.VMEM((held, n_track, 8, q), jnp.float32),
             pltpu.VMEM((n_frame, rows, channels), jnp.float32),
             pltpu.VMEM((n_frame, rows, channels), jnp.float32),
             dma((held, 4)),
@@ -322,8 +322,8 @@
             dma((n_frame,)),
             dma((n_track,)),
             dma((n_track,)),
-            dma((n_track,)),
-            dma((n_track,)),
+            dma((held, n_track)),
+            dma((held, n_track)),
             dma((n_frame,)),
             dma((n_frame,)),
         ],

time: 25.3 us -> 25.4 us (level)
  no operation moved by 1% of the time
where the time goes in v6:
time: 25.4 us; the launch traced here: 25.2 us
  Pallas kernels  21.3 us (84%)
  local copies, waits for them, and re-layouts  2.62 us (10%)
  other arithmetic  0.68 us (3%)
  between operations  0.64 us (3%)
    pallas_call x1, Pallas kernels, on_device(): pl.pallas_call(functools.partial(kernel, n_track, n_frame), out_shape=(ja...  21.3 us
    unnamed x4, local copies, waits for them, and re-layouts  2.62 us
    reshape x1, other arithmetic, on_device(): (query_frame * pixels + query_pixel).astype(jnp.float32).reshape(1, q)  0.68 us

profile of v6, /device:TPU:0, one launch (start us, length us, event | category | flops | bytes accessed | tf_op | source)
XLA Modules:
  0.0 25.2 jit_solution(11904884719107350707)
XLA Ops:
  0.6 0.7 %convert_bitcast_fusion.index_ref = f32[1,128]{1,0:T(1,128)S(1)} fusion(s32[128]{0:T(128)} %param.6, s32[128]{0:T(128)} %param.5), kind=kLoop, calls=%fused_computation | loop fusion | flops 384 | bytes 1536 | tf_op jit(solution)/shard_map/reshape | solution.py:298
  1.3 0.0 copy-start
  1.3 0.7 %copy-done = f32[2,2,128]{2,1,0:T(2,128)S(1)} copy-done((f32[2,2,128]{2,1,0:T(2,128)S(1)}, f32[2,2,128]{2,1,0:T(2,128)}, u32[]{:S(2)}) %copy-start) | copy-done | bytes 2072
  2.0 21.3 %matching_grad.1 = (f32[4096,128]{1,0:T(8,128)S(1)}, f32[32,256]{1,0:T(8,128)S(1)}) custom-call(bf16[2,4096,256]{2,1,0:T(8,128)(2,1)} %frames_hbm.1, f32[1,128]{1,0:T(1,128)S(1)} %convert_bitcast_fusion.index_ref, f32[2,2,128]{2,1,0:T(2,128)S(1)} %copy-done), custom_call_target="tpu_custom_call" | custom-call | tf_op jit(solution)/shard_map/matching_grad/pallas_call | solution.py:301
  23.3 1.3 %copy.9 = f32[1024,2,256]{2,1,0:T(2,128)} copy(f32[1024,2,256]{2,1,0:T(2,128)S(1)} %bitcast.7) | data formatting | bytes 4194304
  24.6 0.6 %copy.10 = f32[32,256]{1,0:T(8,128)} copy(f32[32,256]{1,0:T(8,128)S(1)} %get-tuple-element.9) | data formatting | bytes 65536
Async XLA Ops:
  1.3 0.7 %copy-start = (f32[2,2,128]{2,1,0:T(2,128)S(1)}, f32[2,2,128]{2,1,0:T(2,128)}, u32[]{:S(2)}) copy-start(f32[2,2,128]{2,1,0:T(2,128)} %cot_ref.1) | copy-start | bytes 6148

commit v7 on v6

--- a/solution.py
+++ b/solution.py
@@ -40,8 +40,6 @@
     load_sem,
     pick_send,
     pick_recv,
-    ring_send,
-    ring_recv,
     feat_send,
     feat_recv,
     stat_send,
@@ -99,7 +97,7 @@
     for d, device in frame_peers:
         copies.append(
             pltpu.make_async_remote_copy(
-                src_ref=picked.at[lax.rem(me_f + d, n_frame)],
+                src_ref=picked,
                 dst_ref=picked_in.at[d],
                 send_sem=pick_send.at[d],
                 recv_sem=pick_recv.at[d],
@@ -108,28 +106,12 @@
             )
         )
         copies[-1].start()
-    mine = picked[me_f].astype(jnp.float32)
+    mine = picked[...].astype(jnp.float32)
     for d, copy in enumerate(copies, 1):
         copy.wait_recv()
         mine += picked_in[d].astype(jnp.float32)
-    feats[me_t, me_f] = mine.astype(jnp.bfloat16)
+    feats[me_t] = mine.astype(jnp.bfloat16)
     sends = copies
-    copies = []
-    for d, device in frame_peers:
-        copies.append(
-            pltpu.make_async_remote_copy(
-                src_ref=feats.at[me_t, me_f],
-                dst_ref=feats.at[me_t, me_f],
-                send_sem=ring_send.at[d],
-                recv_sem=ring_recv.at[d],
-                device_id=device,
-                device_id_type=MESH,
-            )
-        )
-        copies[-1].start()
-    for copy in copies:
-        copy.wait_recv()
-    sends += copies
     feat_copies = []
     for d, device in track_peers:
         feat_copies.append(
@@ -310,14 +292,12 @@
             pltpu.VMEM((held, pixels, channels), jnp.bfloat16),
             pltpu.VMEM((held, pixels // wide, q, wide), jnp.float32),
             pltpu.VMEM((n_frame, rows, channels), jnp.bfloat16),
-            pltpu.VMEM((n_frame, rows, channels), jnp.bfloat16),
+            pltpu.VMEM((n_frame, n_frame, rows, channels), jnp.bfloat16),
             pltpu.VMEM((n_track, n_frame, rows, channels), jnp.bfloat16),
             pltpu.VMEM((held, n_track, 8, q), jnp.float32),
             pltpu.VMEM((n_frame, rows, channels), jnp.float32),
             pltpu.VMEM((n_frame, rows, channels), jnp.float32),
             dma((held, 4)),
-            dma((n_frame,)),
-            dma((n_frame,)),
             dma((n_frame,)),
             dma((n_frame,)),
             dma((n_track,)),

time: 25.4 us -> 24.4 us (0.961)
  Pallas kernels: 21.3 us -> 20.3 us
    pallas_call x1, Pallas kernels: 21.3 us -> 20.3 us  [on_device(): pl.pallas_call(functools.partial(kernel, n_track, n_frame), out_shape=(ja...]
where the time goes in v7:
time: 24.4 us; the launch traced here: 24.2 us
  Pallas kernels  20.3 us (83%)
  local copies, waits for them, and re-layouts  2.62 us (11%)
  other arithmetic  0.68 us (3%)
  between operations  0.64 us (3%)
    pallas_call x1, Pallas kernels, on_device(): pl.pallas_call(functools.partial(kernel, n_track, n_frame), out_shape=(ja...  20.3 us
    unnamed x4, local copies, waits for them, and re-layouts  2.62 us
    reshape x1, other arithmetic, on_device(): (query_frame * pixels + query_pixel).astype(jnp.float32).reshape(1, q)  0.68 us

profile of v7, /device:TPU:0, one launch (start us, length us, event | category | flops | bytes accessed | tf_op | source)
XLA Modules:
  0.0 24.2 jit_solution(13166888656560034621)
XLA Ops:
  0.6 0.7 %convert_bitcast_fusion.index_ref = f32[1,128]{1,0:T(1,128)S(1)} fusion(s32[128]{0:T(128)} %param.6, s32[128]{0:T(128)} %param.5), kind=kLoop, calls=%fused_computation | loop fusion | flops 384 | bytes 1536 | tf_op jit(solution)/shard_map/reshape | solution.py:280
  1.3 0.0 copy-start
  1.3 0.7 %copy-done = f32[2,2,128]{2,1,0:T(2,128)S(1)} copy-done((f32[2,2,128]{2,1,0:T(2,128)S(1)}, f32[2,2,128]{2,1,0:T(2,128)}, u32[]{:S(2)}) %copy-start) | copy-done | bytes 2072
  2.0 20.3 %matching_grad.1 = (f32[4096,128]{1,0:T(8,128)S(1)}, f32[32,256]{1,0:T(8,128)S(1)}) custom-call(bf16[2,4096,256]{2,1,0:T(8,128)(2,1)} %frames_hbm.1, f32[1,128]{1,0:T(1,128)S(1)} %convert_bitcast_fusion.index_ref, f32[2,2,128]{2,1,0:T(2,128)S(1)} %copy-done), custom_call_target="tpu_custom_call" | custom-call | tf_op jit(solution)/shard_map/matching_grad/pallas_call | solution.py:283
  22.3 1.3 %copy.9 = f32[1024,2,256]{2,1,0:T(2,128)} copy(f32[1024,2,256]{2,1,0:T(2,128)S(1)} %bitcast.7) | data formatting | bytes 4194304
  23.6 0.6 %copy.10 = f32[32,256]{1,0:T(8,128)} copy(f32[32,256]{1,0:T(8,128)S(1)} %get-tuple-element.9) | data formatting | bytes 65536
Async XLA Ops:
  1.3 0.7 %copy-start = (f32[2,2,128]{2,1,0:T(2,128)S(1)}, f32[2,2,128]{2,1,0:T(2,128)}, u32[]{:S(2)}) copy-start(f32[2,2,128]{2,1,0:T(2,128)} %cot_ref.1) | copy-start | bytes 6148

commit v8 on v7

--- a/solution.py
+++ b/solution.py
@@ -93,41 +93,46 @@
 
     pl.semaphore_wait(barrier, n_track + n_frame - 2)
 
-    copies = []
-    for d, device in frame_peers:
-        copies.append(
-            pltpu.make_async_remote_copy(
-                src_ref=picked,
-                dst_ref=picked_in.at[d],
-                send_sem=pick_send.at[d],
-                recv_sem=pick_recv.at[d],
+    halves = pick_send.shape[0]
+    part = n_frame // halves
+    sends, feat_copies = [], []
+    picks = []
+    for g in range(halves):
+        picks.append([])
+        for d, device in frame_peers:
+            copy = pltpu.make_async_remote_copy(
+                src_ref=picked.at[pl.ds(g * part, part)],
+                dst_ref=picked_in.at[d, pl.ds(g * part, part)],
+                send_sem=pick_send.at[g, d],
+                recv_sem=pick_recv.at[g, d],
                 device_id=device,
                 device_id_type=MESH,
             )
-        )
-        copies[-1].start()
-    mine = picked[...].astype(jnp.float32)
-    for d, copy in enumerate(copies, 1):
-        copy.wait_recv()
-        mine += picked_in[d].astype(jnp.float32)
-    feats[me_t] = mine.astype(jnp.bfloat16)
-    sends = copies
-    feat_copies = []
-    for d, device in track_peers:
-        feat_copies.append(
-            pltpu.make_async_remote_copy(
-                src_ref=feats.at[me_t],
-                dst_ref=feats.at[me_t],
-                send_sem=feat_send.at[d],
-                recv_sem=feat_recv.at[d],
+            copy.start()
+            picks[g].append(copy)
+        sends += picks[g]
+
+    def features(g):
+        where = pl.ds(g * part, part)
+        mine = picked[where].astype(jnp.float32)
+        for d, copy in enumerate(picks[g], 1):
+            copy.wait_recv()
+            mine += picked_in[d, where].astype(jnp.float32)
+        mine = mine.astype(jnp.bfloat16)
+        feats[me_t, where] = mine
+        for d, device in track_peers:
+            copy = pltpu.make_async_remote_copy(
+                src_ref=feats.at[me_t, where],
+                dst_ref=feats.at[me_t, where],
+                send_sem=feat_send.at[g, d],
+                recv_sem=feat_recv.at[g, d],
                 device_id=device,
                 device_id_type=MESH,
             )
-        )
-        feat_copies[-1].start()
-    sends += feat_copies
-
-    own = feats[me_t].reshape(q, channels) * jnp.bfloat16(SCORE_SCALE)
+            copy.start()
+            feat_copies.append(copy)
+        return mine.reshape(part * rows, channels) * jnp.bfloat16(SCORE_SCALE)
+
     wide = scores.shape[3]
     cols = wide // LANES
     chunks = pixels // wide
@@ -142,19 +147,19 @@
     def chunk_of(t, i):
         return fr[t, pl.ds(pl.multiple_of(i * wide, wide), wide), :]
 
-    def scores_step(t, i, peak):
+    def scores_step(g, own, t, i, peak):
         s = dot(own, chunk_of(t, i), ((1,), (1,)))
-        scores[t, i] = s
+        scores[t, i, g * half : (g + 1) * half, :] = s
         return functools.reduce(jnp.maximum, split(s), peak)
 
-    def expo_step(t, i, carry):
+    def expo_step(g, wide_peak, t, i, carry):
         zero, first = carry
-        e = [jnp.exp(part - wide_peaks[t]) for part in split(scores[t, i])]
-        scores[t, i] = jnp.concatenate(e, axis=1)
+        e = [jnp.exp(x - wide_peak) for x in split(scores[t, i, g * half : (g + 1) * half, :])]
+        scores[t, i, g * half : (g + 1) * half, :] = jnp.concatenate(e, axis=1)
         tail = e[-1]
         moment = tail
-        for part in e[-2:0:-1]:
-            tail = tail + part
+        for x in e[-2:0:-1]:
+            tail = tail + x
             moment = moment + tail
         tail = tail + e[0]
         return zero + tail, first + (moment + tail * float(i * cols))
@@ -178,39 +183,49 @@
         slope_y = grad_y * STEP_Y * scale
         return slope_x, slope_y, -(slope_x * mean_x + slope_y * mean_y)
 
-    peaks, wide_peaks, columns, lines_of, stat_copies = {}, {}, {}, {}, []
+    half = q // halves
+    peaks, sums, lines_of, stat_copies = {}, {}, {}, []
+    empty = jnp.zeros((half, LANES), jnp.float32)
+    for g in range(halves):
+        own = features(g)
+        for turn in range(held + 1):
+            peak = jnp.full((half, LANES), -jnp.inf, jnp.float32)
+            carry = (empty, empty)
+            if turn > 0:
+                wide_peak = jnp.broadcast_to(peaks[g, turn - 1], (half, LANES))
+            for i in range(chunks):
+                if turn < held:
+                    peak = scores_step(g, own, turn, i, peak)
+                if turn > 0:
+                    carry = expo_step(g, wide_peak, turn - 1, i, carry)
+            if turn < held:
+                peaks[g, turn] = jnp.max(peak, axis=1, keepdims=True)
+            if turn > 0:
+                sums[g, turn - 1] = carry
+    for t in range(held):
+        zero, first = [jnp.concatenate([sums[g, t][j] for g in range(halves)], axis=0) for j in range(2)]
+        peak = jnp.concatenate([peaks[g, t] for g in range(halves)], axis=0)
+        slope_x, slope_y, level = softmax_terms(t, zero, first)
+        step = jnp.broadcast_to(slope_y, (q, LANES))
+        lines_of[t] = (level + slope_x * lane_x + step * lane_y, step * row_step)
+        rest = [to_row(column) for column in (peak, slope_x, slope_y, level)]
+        stats[t, me_t] = jnp.concatenate(rest + rest, axis=0)
+        for d, device in track_peers:
+            copy = pltpu.make_async_remote_copy(
+                src_ref=stats.at[t, me_t],
+                dst_ref=stats.at[t, me_t],
+                send_sem=stat_send.at[t, d],
+                recv_sem=stat_recv.at[t, d],
+                device_id=device,
+                device_id_type=MESH,
+            )
+            copy.start()
+            stat_copies.append(copy)
+    sends += feat_copies
     total = jnp.zeros((q, channels), jnp.float32)
-    empty = jnp.zeros((q, LANES), jnp.float32)
-    for turn in range(held + 2):
-        peak = jnp.full((q, LANES), -jnp.inf, jnp.float32)
-        sums = (empty, empty)
+    for t in range(held):
         for i in range(chunks):
-            if turn < held:
-                peak = scores_step(turn, i, peak)
-            if 0 <= turn - 1 < held:
-                sums = expo_step(turn - 1, i, sums)
-            if 0 <= turn - 2 < held:
-                total = query_step(turn - 2, i, total)
-        if turn < held:
-            peaks[turn] = jnp.max(peak, axis=1, keepdims=True)
-            wide_peaks[turn] = jnp.broadcast_to(peaks[turn], (q, LANES))
-        if 0 <= turn - 1 < held:
-            slope_x, slope_y, level = columns[turn - 1] = softmax_terms(turn - 1, *sums)
-            step = jnp.broadcast_to(slope_y, (q, LANES))
-            lines_of[turn - 1] = (level + slope_x * lane_x + step * lane_y, step * row_step)
-            rest = [to_row(column) for column in (peaks[turn - 1],) + columns[turn - 1]]
-            stats[turn - 1, me_t] = jnp.concatenate(rest + rest, axis=0)
-            for d, device in track_peers:
-                copy = pltpu.make_async_remote_copy(
-                    src_ref=stats.at[turn - 1, me_t],
-                    dst_ref=stats.at[turn - 1, me_t],
-                    send_sem=stat_send.at[turn - 1, d],
-                    recv_sem=stat_recv.at[turn - 1, d],
-                    device_id=device,
-                    device_id_type=MESH,
-                )
-                copy.start()
-                stat_copies.append(copy)
+            total = query_step(t, i, total)
     sends += stat_copies
 
     term[...] = total.reshape(n_frame, rows, channels)
@@ -277,6 +292,7 @@
     block = pixels // n_track
     tiles = channels // LANES
     wide = 4 * LANES
+    halves = 2 if n_frame % 2 == 0 and (q // 2) % 16 == 0 else 1
     index = (query_frame * pixels + query_pixel).astype(jnp.float32).reshape(1, q)
     vmem = pl.BlockSpec(memory_space=pltpu.VMEM)
     dma = pltpu.SemaphoreType.DMA
@@ -298,10 +314,10 @@
             pltpu.VMEM((n_frame, rows, channels), jnp.float32),
             pltpu.VMEM((n_frame, rows, channels), jnp.float32),
             dma((held, 4)),
-            dma((n_frame,)),
-            dma((n_frame,)),
-            dma((n_track,)),
-            dma((n_track,)),
+            dma((halves, n_frame)),
+            dma((halves, n_frame)),
+            dma((halves, n_track)),
+            dma((halves, n_track)),
             dma((held, n_track)),
             dma((held, n_track)),
             dma((n_frame,)),

time: 24.4 us -> 25.7 us (1.053)
  Pallas kernels: 20.3 us -> 21.5 us
    pallas_call x1, Pallas kernels: 20.3 us -> 21.5 us  [on_device(): pl.pallas_call(functools.partial(kernel, n_track, n_frame), out_shape=(ja...]
where the time goes in v8:
time: 25.7 us; the launch traced here: 25.5 us
  Pallas kernels  21.5 us (84%)
  local copies, waits for them, and re-layouts  2.62 us (10%)
  other arithmetic  0.68 us (3%)
  between operations  0.64 us (2%)
    pallas_call x1, Pallas kernels, on_device(): pl.pallas_call(functools.partial(kernel, n_track, n_frame), out_shape=(ja...  21.5 us
    unnamed x4, local copies, waits for them, and re-layouts  2.62 us
    reshape x1, other arithmetic, on_device(): (query_frame * pixels + query_pixel).astype(jnp.float32).reshape(1, q)  0.68 us

profile of v8, /device:TPU:0, one launch (start us, length us, event | category | flops | bytes accessed | tf_op | source)
XLA Modules:
  0.0 25.5 jit_solution(6135950690421726626)
XLA Ops:
  0.6 0.7 %convert_bitcast_fusion.index_ref = f32[1,128]{1,0:T(1,128)S(1)} fusion(s32[128]{0:T(128)} %param.6, s32[128]{0:T(128)} %param.5), kind=kLoop, calls=%fused_computation | loop fusion | flops 384 | bytes 1536 | tf_op jit(solution)/shard_map/reshape | solution.py:296
  1.3 0.0 copy-start
  1.3 0.7 %copy-done = f32[2,2,128]{2,1,0:T(2,128)S(1)} copy-done((f32[2,2,128]{2,1,0:T(2,128)S(1)}, f32[2,2,128]{2,1,0:T(2,128)}, u32[]{:S(2)}) %copy-start) | copy-done | bytes 2072
  2.0 21.5 %matching_grad.1 = (f32[4096,128]{1,0:T(8,128)S(1)}, f32[32,256]{1,0:T(8,128)S(1)}) custom-call(bf16[2,4096,256]{2,1,0:T(8,128)(2,1)} %frames_hbm.1, f32[1,128]{1,0:T(1,128)S(1)} %convert_bitcast_fusion.index_ref, f32[2,2,128]{2,1,0:T(2,128)S(1)} %copy-done), custom_call_target="tpu_custom_call" | custom-call | tf_op jit(solution)/shard_map/matching_grad/pallas_call | solution.py:299
  23.5 1.3 %copy.9 = f32[1024,2,256]{2,1,0:T(2,128)} copy(f32[1024,2,256]{2,1,0:T(2,128)S(1)} %bitcast.7) | data formatting | bytes 4194304
  24.9 0.6 %copy.10 = f32[32,256]{1,0:T(8,128)} copy(f32[32,256]{1,0:T(8,128)S(1)} %get-tuple-element.9) | data formatting | bytes 65536
Async XLA Ops:
  1.3 0.7 %copy-start = (f32[2,2,128]{2,1,0:T(2,128)S(1)}, f32[2,2,128]{2,1,0:T(2,128)}, u32[]{:S(2)}) copy-start(f32[2,2,128]{2,1,0:T(2,128)} %cot_ref.1) | copy-start | bytes 6148

commit v9 on v7

--- a/solution.py
+++ b/solution.py
@@ -276,7 +276,7 @@
     rows = q // n_frame
     block = pixels // n_track
     tiles = channels // LANES
-    wide = 4 * LANES
+    wide = 8 * LANES
     index = (query_frame * pixels + query_pixel).astype(jnp.float32).reshape(1, q)
     vmem = pl.BlockSpec(memory_space=pltpu.VMEM)
     dma = pltpu.SemaphoreType.DMA

time: 24.4 us -> 24.4 us (level)
  no operation moved by 1% of the time
where the time goes in v9:
time: 24.4 us; the launch traced here: 24.2 us
  Pallas kernels  20.3 us (83%)
  local copies, waits for them, and re-layouts  2.62 us (11%)
  other arithmetic  0.68 us (3%)
  between operations  0.64 us (3%)
    pallas_call x1, Pallas kernels, on_device(): pl.pallas_call(functools.partial(kernel, n_track, n_frame), out_shape=(ja...  20.3 us
    unnamed x4, local copies, waits for them, and re-layouts  2.62 us
    reshape x1, other arithmetic, on_device(): (query_frame * pixels + query_pixel).astype(jnp.float32).reshape(1, q)  0.68 us

profile of v9, /device:TPU:0, one launch (start us, length us, event | category | flops | bytes accessed | tf_op | source)
XLA Modules:
  0.0 24.2 jit_solution(15633290714193210963)
XLA Ops:
  0.6 0.7 %convert_bitcast_fusion.index_ref = f32[1,128]{1,0:T(1,128)S(1)} fusion(s32[128]{0:T(128)} %param.6, s32[128]{0:T(128)} %param.5), kind=kLoop, calls=%fused_computation | loop fusion | flops 384 | bytes 1536 | tf_op jit(solution)/shard_map/reshape | solution.py:280
  1.3 0.0 copy-start
  1.3 0.7 %copy-done = f32[2,2,128]{2,1,0:T(2,128)S(1)} copy-done((f32[2,2,128]{2,1,0:T(2,128)S(1)}, f32[2,2,128]{2,1,0:T(2,128)}, u32[]{:S(2)}) %copy-start) | copy-done | bytes 2072
  2.0 20.3 %matching_grad.1 = (f32[4096,128]{1,0:T(8,128)S(1)}, f32[32,256]{1,0:T(8,128)S(1)}) custom-call(bf16[2,4096,256]{2,1,0:T(8,128)(2,1)} %frames_hbm.1, f32[1,128]{1,0:T(1,128)S(1)} %convert_bitcast_fusion.index_ref, f32[2,2,128]{2,1,0:T(2,128)S(1)} %copy-done), custom_call_target="tpu_custom_call" | custom-call | tf_op jit(solution)/shard_map/matching_grad/pallas_call | solution.py:283
  22.3 1.3 %copy.9 = f32[1024,2,256]{2,1,0:T(2,128)} copy(f32[1024,2,256]{2,1,0:T(2,128)S(1)} %bitcast.7) | data formatting | bytes 4194304
  23.6 0.6 %copy.10 = f32[32,256]{1,0:T(8,128)} copy(f32[32,256]{1,0:T(8,128)S(1)} %get-tuple-element.9) | data formatting | bytes 65536
Async XLA Ops:
  1.3 0.7 %copy-start = (f32[2,2,128]{2,1,0:T(2,128)S(1)}, f32[2,2,128]{2,1,0:T(2,128)}, u32[]{:S(2)}) copy-start(f32[2,2,128]{2,1,0:T(2,128)} %cot_ref.1) | copy-start | bytes 6148
